TPU v7x, 32 devices: a whole 2x2x4 slice. The times are simulated.
32 devices in a mesh: head: 4 (over z), batch: 8 (over y, x, core).
Axes of the slice: x: 2, y: 2, z: 4, core: 2. Of those that a mesh axis runs over, the one named last changes fastest.
Arguments:
- layer_input: bfloat16 [8192, 1024], P(('batch', 'head')), may hold values from -6 to 6
- cotangent: bfloat16 [8192, 1024], P(('batch', 'head')), may hold values from -6 to 6
- segments: int32 [8192], P('batch'), may hold values from 0 to 126, as said below
- mix_gain: float32 [1024], replicated, may hold values from 0.5 to 1.5
- query_weight: bfloat16 [1024, 1024], P('batch', 'head'), may hold values from -0.1875 to 0.1875
- key_weight: bfloat16 [1024, 2048], P('batch', 'head'), may hold values from -0.1875 to 0.1875
- value_weight: bfloat16 [1024, 2048], P('batch', 'head'), may hold values from -0.1875 to 0.1875
- outgate_weight: bfloat16 [1024, 1024], P('batch', 'head'), may hold values from -0.1875 to 0.1875
- rate_weight: bfloat16 [1024, 24], P('batch', 'head'), may hold values from -0.1875 to 0.1875
- conv_query: float32 [4, 1024], replicated, may hold values from -3 to 3
- conv_key: float32 [4, 2048], replicated, may hold values from -3 to 3
- conv_value: float32 [4, 2048], replicated, may hold values from -3 to 3
- decay_bias: float32 [8], replicated, may hold values from -4 to 1
- out_gain: float32 [128], replicated, may hold values from 0.5 to 1.5
- out_weight: bfloat16 [1024, 1024], P('head', 'batch'), may hold values from -0.1875 to 0.1875
- mlp_gain: float32 [1024], replicated, may hold values from 0.5 to 1.5
- gate_weight: bfloat16 [1024, 2816], P('batch', 'head'), may hold values from -0.1875 to 0.1875
- up_weight: bfloat16 [1024, 2816], P('batch', 'head'), may hold values from -0.1875 to 0.1875
- down_weight: bfloat16 [2816, 1024], P('head', 'batch'), may hold values from -0.109375 to 0.109375
Outputs:
- layer_output: bfloat16 [8192, 1024], P(('batch', 'head'))
- input_grad: float32 [8192, 1024], P(('batch', 'head'))
- mix_gain_grad: float32 [1024], replicated
- query_weight_grad: float32 [1024, 1024], P('batch', 'head')
- key_weight_grad: float32 [1024, 2048], P('batch', 'head')
- value_weight_grad: float32 [1024, 2048], P('batch', 'head')
- outgate_weight_grad: float32 [1024, 1024], P('batch', 'head')
- rate_weight_grad: float32 [1024, 24], P('batch', 'head')
- conv_query_grad: float32 [4, 1024], replicated
- conv_key_grad: float32 [4, 2048], replicated
- conv_value_grad: float32 [4, 2048], replicated
- decay_bias_grad: float32 [8], replicated
- out_gain_grad: float32 [128], replicated
- out_weight_grad: float32 [1024, 1024], P('head', 'batch')
- mlp_gain_grad: float32 [1024], replicated
- gate_weight_grad: float32 [1024, 2816], P('batch', 'head')
- up_weight_grad: float32 [1024, 2816], P('batch', 'head')
- down_weight_grad: float32 [2816, 1024], P('head', 'batch')
Inputs may be any that keep to these rules, and one draw needn't show every extreme that they name: `segments`: segment ids count documents within each packed row of 1024 tokens: they are 0 at the row's first token and rise by one at each document's first token; documents begin only before position max(64, 1) or after position 1024 - max(64, 1), so in every row one document covers the positions between; in some row every one of those edge positions begins a document.
All inputs are finite; a program needn't handle non-finite values.
Results may differ from a plain program's by a relative error of at most 0.013.
The roundings to bfloat16 on the way count: a program that leaves them out, or rounds other values in their place, can miss the bound.
Values may be sent and summed in bfloat16 or wider, within the bound.
No kernel may reach another device: no remote copies, remote signals or barrier semaphores. Data moves between devices by JAX's collectives and lax.ppermute only.
A program may use at most 320 MiB of HBM per device.

v0:
```python
from functools import partial
import math

import jax
import jax.numpy as jnp
from jax import lax
from jax.sharding import PartitionSpec as P

HEAD_DIM = 128


EPS = 1e-06
EXACT_PRECISION = lax.Precision.HIGHEST


def dot_rows(left, right):
    return lax.dot_general(
        left, right, (((0,), (0,)), ((), ())), preferred_element_type=jnp.float32
    )


def dot_cols(left, right):
    return lax.dot_general(
        left, right, (((1,), (1,)), ((), ())), preferred_element_type=jnp.float32
    )


def row_norm(values, gain):
    scale = lax.rsqrt(jnp.mean(values * values, axis=-1, keepdims=True) + EPS)
    return (values * scale * gain, scale)


def norm_back(grad, values, scale, gain):
    normed = values * scale
    gain_grad = jnp.sum(grad * normed, axis=0)
    weighted = grad * gain
    value_grad = scale * (weighted - normed * jnp.mean(weighted * normed, axis=-1, keepdims=True))
    return (value_grad, gain_grad)


def unit_norm(values):
    return values * lax.rsqrt(jnp.sum(values * values, axis=-1, keepdims=True) + EPS)


def short_conv(raw_cols, taps, segments):
    length = raw_cols.shape[0]
    total = raw_cols * taps[0]
    for offset in range(1, taps.shape[0]):
        shifted = jnp.pad(raw_cols, ((offset, 0), (0, 0)))[:length]
        earlier = jnp.pad(segments, (offset, 0), constant_values=-1)[:length]
        total = total + jnp.where((earlier == segments)[:, None], shifted, 0.0) * taps[offset]
    return total


def to_blocks(array, count):
    local_heads = array.shape[1]
    merged = jnp.swapaxes(array, 0, 1).reshape((local_heads, count, -1) + array.shape[3:])
    return jnp.swapaxes(merged, 0, 1)


def delta_product(query_rows, keys, values, betas, log_keep, segments, block_len):
    length, local_heads, width = query_rows.shape
    span = 2 * block_len
    count = 2 * length // span
    block_keys = to_blocks(keys, count)
    block_values = to_blocks(values, count)
    block_query = to_blocks(
        jnp.broadcast_to(query_rows[:, :, None, :], (length, local_heads, 2, width)), count
    )
    block_beta = to_blocks(betas, count)
    block_log = to_blocks(jnp.stack([log_keep, jnp.zeros_like(log_keep)], axis=-1), count)
    block_seg = jnp.repeat(segments, 2).reshape(count, span)
    index = jnp.arange(span)
    lower = index[:, None] > index[None, :]
    lower_eq = index[:, None] >= index[None, :]
    ident = jnp.eye(span, dtype=jnp.float32)

    def stretch_step(carry, block):
        memory_state, last_seg = carry
        block_key_rows, bvalues, block_query_rows, bbeta, blog, bseg = block
        cumul = jnp.cumsum(blog, axis=1)
        same = (bseg[:, None] == bseg[None, :]) & lower_eq
        spread = jnp.where(same, cumul[:, :, None] - cumul[:, None, :], 0.0)
        decay = jnp.where(same, jnp.exp(spread), 0.0)
        start_keep = jnp.where(bseg == last_seg, jnp.exp(cumul), 0.0)
        final_keep_factor = jnp.where(bseg == bseg[-1], jnp.exp(cumul[:, -1:] - cumul), 0.0)
        total_keep = jnp.where(bseg[-1] == last_seg, jnp.exp(cumul[:, -1]), 0.0)
        key_dots = jnp.einsum(
            "hik,hjk->hij", block_key_rows, block_key_rows, precision=EXACT_PRECISION
        )
        system = ident + jnp.where(lower, bbeta[:, :, None] * decay * key_dots, 0.0)
        recalled_values = jnp.einsum(
            "eyr,erm->eym", block_key_rows, memory_state, precision=EXACT_PRECISION
        )
        right_side = bbeta[:, :, None] * (bvalues - start_keep[:, :, None] * recalled_values)
        proxy_output = jax.scipy.linalg.solve_triangular(
            system, right_side, lower=True, unit_diagonal=True
        )
        scores = (
            jnp.einsum("hik,hjk->hij", block_query_rows, block_key_rows, precision=EXACT_PRECISION)
            * decay
        )
        outputs = start_keep[:, :, None] * jnp.einsum(
            "eyr,erm->eym", block_query_rows, memory_state, precision=EXACT_PRECISION
        )
        outputs = outputs + jnp.einsum(
            "hij,hjv->hiv", scores, proxy_output, precision=EXACT_PRECISION
        )
        new_memory = total_keep[:, None, None] * memory_state + jnp.einsum(
            "mzt,mza->mta",
            block_key_rows * final_keep_factor[:, :, None],
            proxy_output,
            precision=EXACT_PRECISION,
        )
        return ((new_memory, bseg[-1]), outputs)

    start = (jnp.zeros((local_heads, width, width), jnp.float32), jnp.int32(-1))
    final_carry, outputs = lax.scan(
        stretch_step,
        start,
        (block_keys, block_values, block_query, block_beta, block_log, block_seg),
    )
    outputs = jnp.swapaxes(outputs, 0, 1).reshape(local_heads, length, 2, width)[:, :, 1]
    return jnp.swapaxes(outputs, 0, 1)


def mixer_local(
    query_raw,
    key_raw,
    value_raw,
    outgate_raw,
    rate_raw,
    conv_query,
    conv_key,
    conv_value,
    decay_bias,
    out_gain,
    segments,
    block_len,
):
    length = query_raw.shape[0]
    local_heads = decay_bias.shape[0]
    width = out_gain.shape[0]
    query_rows = unit_norm(
        jax.nn.silu(short_conv(query_raw, conv_query, segments)).reshape(length, local_heads, width)
    )
    keys = unit_norm(
        jax.nn.silu(short_conv(key_raw, conv_key, segments)).reshape(length, local_heads, 2, width)
    )
    values = jax.nn.silu(short_conv(value_raw, conv_value, segments)).reshape(
        length, local_heads, 2, width
    )
    rates = rate_raw.reshape(length, local_heads, 3)
    betas = jax.nn.sigmoid(rates[:, :, 0:2])
    log_keep = -jax.nn.softplus(rates[:, :, 2] + decay_bias)
    recalls = delta_product(query_rows, keys, values, betas, log_keep, segments, block_len)
    scale = lax.rsqrt(jnp.mean(recalls * recalls, axis=-1, keepdims=True) + EPS)
    gate = jax.nn.silu(outgate_raw.reshape(length, local_heads, width))
    return (recalls * scale * out_gain * gate).reshape(length, local_heads * width)


def swiglu_back(hidden_grad, gate_pre, up_pre):
    gate_sigmoid = jax.nn.sigmoid(gate_pre)
    gate_grad = hidden_grad * up_pre * gate_sigmoid * (1.0 + gate_pre * (1.0 - gate_sigmoid))
    up_grad = hidden_grad * gate_pre * gate_sigmoid
    return (gate_grad.astype(jnp.bfloat16), up_grad.astype(jnp.bfloat16))


def body(
    layer_input,
    cotangent,
    segments,
    mix_gain,
    query_weight,
    key_weight,
    value_weight,
    outgate_weight,
    rate_weight,
    conv_query,
    conv_key,
    conv_value,
    decay_bias,
    out_gain,
    out_weight,
    mlp_gain,
    gate_weight,
    up_weight,
    down_weight,
):
    head_index = lax.axis_index("head")
    local_rows = layer_input.shape[0]
    query_w, key_w, value_w, outgate_w, rate_w, out_w, gate_w, up_w, down_w = (
        lax.all_gather(query_weight, "batch", axis=0, tiled=True),
        lax.all_gather(key_weight, "batch", axis=0, tiled=True),
        lax.all_gather(value_weight, "batch", axis=0, tiled=True),
        lax.all_gather(outgate_weight, "batch", axis=0, tiled=True),
        lax.all_gather(rate_weight, "batch", axis=0, tiled=True),
        lax.all_gather(out_weight, "batch", axis=1, tiled=True),
        lax.all_gather(gate_weight, "batch", axis=0, tiled=True),
        lax.all_gather(up_weight, "batch", axis=0, tiled=True),
        lax.all_gather(down_weight, "batch", axis=1, tiled=True),
    )
    local_heads = query_w.shape[1] // HEAD_DIM

    def head_cols(table, per_head):
        return lax.dynamic_slice_in_dim(
            table, head_index * local_heads * per_head, local_heads * per_head, axis=table.ndim - 1
        )

    resid_in = layer_input.astype(jnp.float32)
    normed_in, scale_in = row_norm(resid_in, mix_gain)
    rows_in = lax.all_gather(normed_in.astype(jnp.bfloat16), "head", axis=0, tiled=True)
    proj_weights = (query_w, key_w, value_w, outgate_w, rate_w)
    projections = [
        jnp.dot(rows_in, weight, preferred_element_type=jnp.float32) for weight in proj_weights
    ]
    block_len = math.gcd(rows_in.shape[0], 256)
    mixer = partial(mixer_local, segments=segments, block_len=block_len)
    mixed_heads, mixer_back = jax.vjp(
        mixer,
        projections[0],
        projections[1],
        projections[2],
        projections[3],
        projections[4],
        head_cols(conv_query, HEAD_DIM),
        head_cols(conv_key, 2 * HEAD_DIM),
        head_cols(conv_value, 2 * HEAD_DIM),
        head_cols(decay_bias, 1),
        out_gain,
    )
    mixed_low = mixed_heads.astype(jnp.bfloat16)
    resid_mid = resid_in + lax.psum_scatter(
        jnp.dot(mixed_low, out_w, preferred_element_type=jnp.float32),
        "head",
        scatter_dimension=0,
        tiled=True,
    )
    normed_mid, scale_mid = row_norm(resid_mid, mlp_gain)
    normed_mid_low = normed_mid.astype(jnp.bfloat16)
    grad_out = cotangent.astype(jnp.float32)
    rows_mid = lax.all_gather(normed_mid_low, "head", axis=0, tiled=True)
    gate_pre = jnp.dot(rows_mid, gate_w, preferred_element_type=jnp.float32)
    up_pre = jnp.dot(rows_mid, up_w, preferred_element_type=jnp.float32)
    hidden = (jax.nn.silu(gate_pre) * up_pre).astype(jnp.bfloat16)
    layer_output = (
        resid_mid
        + lax.psum_scatter(
            jnp.dot(hidden, down_w, preferred_element_type=jnp.float32).astype(jnp.bfloat16),
            "head",
            scatter_dimension=0,
            tiled=True,
        ).astype(jnp.float32)
    ).astype(jnp.bfloat16)
    rows_grad = lax.all_gather(cotangent, "head", axis=0, tiled=True)
    hidden_grad = dot_cols(rows_grad, down_w)
    gate_grad, up_grad = swiglu_back(hidden_grad, gate_pre, up_pre)
    mid_grad = lax.psum_scatter(
        dot_cols(gate_grad, gate_w) + dot_cols(up_grad, up_w),
        "head",
        scatter_dimension=0,
        tiled=True,
    )
    gate_total, up_total, down_total = (
        lax.psum_scatter(
            dot_rows(rows_mid, gate_grad).astype(jnp.bfloat16),
            "batch",
            scatter_dimension=0,
            tiled=True,
        ).astype(jnp.float32),
        lax.psum_scatter(
            dot_rows(rows_mid, up_grad).astype(jnp.bfloat16),
            "batch",
            scatter_dimension=0,
            tiled=True,
        ).astype(jnp.float32),
        lax.psum_scatter(
            dot_rows(hidden, rows_grad).astype(jnp.bfloat16),
            "batch",
            scatter_dimension=1,
            tiled=True,
        ).astype(jnp.float32),
    )
    mid_back, mlp_gain_part = norm_back(mid_grad, resid_mid, scale_mid, mlp_gain)
    resid_grad = grad_out + mid_back
    rows_resid_grad = lax.all_gather(resid_grad.astype(jnp.bfloat16), "head", axis=0, tiled=True)
    mixed_grad = dot_cols(rows_resid_grad, out_w)
    out_sum = dot_rows(mixed_low, rows_resid_grad)
    back_terms = mixer_back(mixed_grad)
    raw_low = [grad.astype(jnp.bfloat16) for grad in back_terms[0:5]]
    proj_sums = [dot_rows(rows_in, grad) for grad in raw_low]
    total = jnp.zeros((local_rows * lax.axis_size("head"), rows_in.shape[1]), jnp.float32)
    for grad, weight in zip(raw_low, proj_weights):
        total = total + dot_cols(grad, weight)
    in_grad = lax.psum_scatter(
        total.astype(jnp.bfloat16), "head", scatter_dimension=0, tiled=True
    ).astype(jnp.float32)
    in_back, mix_gain_part = norm_back(in_grad, resid_in, scale_in, mix_gain)
    input_grad = resid_grad + in_back
    query_sum, key_sum, value_sum, outgate_sum, rate_sum, out_total = (
        lax.psum_scatter(
            proj_sums[0].astype(jnp.bfloat16), "batch", scatter_dimension=0, tiled=True
        ).astype(jnp.float32),
        lax.psum_scatter(
            proj_sums[1].astype(jnp.bfloat16), "batch", scatter_dimension=0, tiled=True
        ).astype(jnp.float32),
        lax.psum_scatter(
            proj_sums[2].astype(jnp.bfloat16), "batch", scatter_dimension=0, tiled=True
        ).astype(jnp.float32),
        lax.psum_scatter(
            proj_sums[3].astype(jnp.bfloat16), "batch", scatter_dimension=0, tiled=True
        ).astype(jnp.float32),
        lax.psum_scatter(
            proj_sums[4].astype(jnp.bfloat16), "batch", scatter_dimension=0, tiled=True
        ).astype(jnp.float32),
        lax.psum_scatter(
            out_sum.astype(jnp.bfloat16), "batch", scatter_dimension=1, tiled=True
        ).astype(jnp.float32),
    )

    def place_cols(table_shape, local_part, per_head):
        return lax.dynamic_update_slice_in_dim(
            jnp.zeros(table_shape, jnp.float32),
            local_part,
            head_index * local_heads * per_head,
            axis=len(table_shape) - 1,
        )

    (
        mix_gain_grad,
        mlp_gain_grad,
        out_gain_grad,
        conv_query_grad,
        conv_key_grad,
        conv_value_grad,
        decay_bias_grad,
    ) = lax.psum(
        (
            mix_gain_part,
            mlp_gain_part,
            back_terms[9],
            place_cols(conv_query.shape, back_terms[5], HEAD_DIM),
            place_cols(conv_key.shape, back_terms[6], 2 * HEAD_DIM),
            place_cols(conv_value.shape, back_terms[7], 2 * HEAD_DIM),
            place_cols(decay_bias.shape, back_terms[8], 1),
        ),
        ("head", "batch"),
    )
    return (
        layer_output,
        input_grad,
        mix_gain_grad,
        query_sum,
        key_sum,
        value_sum,
        outgate_sum,
        rate_sum,
        conv_query_grad,
        conv_key_grad,
        conv_value_grad,
        decay_bias_grad,
        out_gain_grad,
        out_total,
        mlp_gain_grad,
        gate_total,
        up_total,
        down_total,
    )


def solution(mesh):
    placed = (
        P(("batch", "head"), None),
        P(("batch", "head"), None),
        P("batch"),
        P(),
        P("batch", "head"),
        P("batch", "head"),
        P("batch", "head"),
        P("batch", "head"),
        P("batch", "head"),
        P(),
        P(),
        P(),
        P(),
        P(),
        P("head", "batch"),
        P(),
        P("batch", "head"),
        P("batch", "head"),
        P("head", "batch"),
    )
    return jax.shard_map(
        body,
        mesh=mesh,
        in_specs=placed,
        out_specs=(
            P(("batch", "head"), None),
            P(("batch", "head"), None),
            P(),
            P("batch", "head"),
            P("batch", "head"),
            P("batch", "head"),
            P("batch", "head"),
            P("batch", "head"),
            P(),
            P(),
            P(),
            P(),
            P(),
            P("head", "batch"),
            P(),
            P("batch", "head"),
            P("batch", "head"),
            P("head", "batch"),
        ),
        check_vma=False,
    )
```

profile of v0, /device:TPU:0, one launch (start us, length us, event | category | flops | bytes accessed | tf_op | source)
XLA Modules:
  0.0 2389.1 jit_solution(7081323576962186357)
XLA Ops:
  58.2 27.5 %all-gather.10.cloned.1.call-done = bf16[1024,1024]{1,0:T(8,128)(2,1)} async-done(((bf16[256,1024]{1,0:T(8,128)(2,1)}), bf16[1024,1024]{1,0:T(8,128)(2,1)}) %all-gather.10.cloned.1.call-update) | async-done | bytes 2097168 | tf_op jit(solution)/shard_map/all_gather | solution.py:212
  90.3 19.5 all-gather.14.cloned.1.call-done
  153.7 581.5 %while.104 = (s32[]{:T(128)}, f32[2,128,128]{2,1,0:T(8,128)S(1)}, s32[]{:T(128)}, f32[4,2,512,128]{3,2,0,1:T(8,128)}, pred[4,2,512,512]{3,2,1,0:T(32,128)(4,1)},...) while((s32[]{:T(128)}, f32[2,128,128]{2,1,0:T(8,128)S(1)}, ...), condition=%wide.region_6.7_spmd.clone, body=%wide.region_3.6_spmd.clone.sunk | while | flops 3541476864 | bytes 54855112 | solution.py:118
  175.9 14.8 while.107
  190.7 80.1 %custom-call.45 = f32[2,4,128,128]{2,3,1,0:T(8,128)} custom-call(f32[2,4,128,128]{3,2,1,0:T(8,128)} %bitcast.768), custom_call_target="InvertDiagBlocksLowerTriangular" | custom-call | tf_op jit(solution)/shard_map/jvp()/while/body/eval_jaxpr/jit(_solve_triangular)/vmap()/triangular_solve | solution.py:96
  320.5 14.8 while.107
  335.3 80.1 %custom-call.45 = f32[2,4,128,128]{2,3,1,0:T(8,128)} custom-call(f32[2,4,128,128]{3,2,1,0:T(8,128)} %bitcast.768), custom_call_target="InvertDiagBlocksLowerTriangular" | custom-call | tf_op jit(solution)/shard_map/jvp()/while/body/eval_jaxpr/jit(_solve_triangular)/vmap()/triangular_solve | solution.py:96
  466.0 14.8 while.107
  480.8 80.1 %custom-call.45 = f32[2,4,128,128]{2,3,1,0:T(8,128)} custom-call(f32[2,4,128,128]{3,2,1,0:T(8,128)} %bitcast.768), custom_call_target="InvertDiagBlocksLowerTriangular" | custom-call | tf_op jit(solution)/shard_map/jvp()/while/body/eval_jaxpr/jit(_solve_triangular)/vmap()/triangular_solve | solution.py:96
  611.5 14.8 while.107
  626.3 80.1 %custom-call.45 = f32[2,4,128,128]{2,3,1,0:T(8,128)} custom-call(f32[2,4,128,128]{3,2,1,0:T(8,128)} %bitcast.768), custom_call_target="InvertDiagBlocksLowerTriangular" | custom-call | tf_op jit(solution)/shard_map/jvp()/while/body/eval_jaxpr/jit(_solve_triangular)/vmap()/triangular_solve | solution.py:96
  745.6 76.3 %reduce-scatter.24.cloned.1.call-done = f32[256,1024]{1,0:T(8,128)} async-done(((f32[1024,1024]{1,0:T(8,128)}), f32[256,1024]{1,0:T(8,128)}) %reduce-scatter.24.cloned.1.call-update) | async-done | bytes 1048592 | tf_op jit(solution)/shard_map/reduce_scatter | solution.py:233
  826.9 22.6 all-gather.18.cloned.1.call-done
  849.6 48.0 %all-gather.16.cloned.1.call-done = bf16[1024,1024]{1,0:T(8,128)(2,1)} async-done(((bf16[256,1024]{1,0:T(8,128)(2,1)}), bf16[1024,1024]{1,0:T(8,128)(2,1)}) %all-gather.16.cloned.1.call-update) | async-done | bytes 2097168 | tf_op jit(solution)/shard_map/all_gather | solution.py:242
  902.8 20.8 all-gather.20.cloned.1.call-done
  928.9 22.1 all-gather.22.cloned.1.call-done
  951.0 47.6 %all-gather.24.cloned.1.call-done = bf16[1024,1024]{1,0:T(8,128)(2,1)} async-done(((bf16[256,1024]{1,0:T(8,128)(2,1)}), bf16[1024,1024]{1,0:T(8,128)(2,1)}) %all-gather.24.cloned.1.call-update) | async-done | bytes 2097168 | tf_op jit(solution)/shard_map/all_gather | solution.py:255
  1012.9 75.6 %reduce-scatter.28.cloned.1.call-done = f32[256,1024]{1,0:T(8,128)} async-done(((f32[1024,1024]{1,0:T(8,128)}), f32[256,1024]{1,0:T(8,128)}) %reduce-scatter.28.cloned.1.call-update) | async-done | bytes 1048592 | tf_op jit(solution)/shard_map/reduce_scatter | solution.py:258
  1115.6 23.5 all-gather.26.cloned.1.call-done
  1154.5 748.5 %while.106 = (s32[]{:T(128)}, f32[2,128,128]{2,1,0:T(8,128)}, f32[4,2,512,128]{3,2,0,1:T(8,128)}, f32[4,2,512,128]{3,2,0,1:T(8,128)}, f32[4,2,512,128]{3,2,0,1:T...) while((s32[]{:T(128)}, f32[2,128,128]{2,1,0:T(8,128)}, ...), condition=%wide.region_26.28_spmd.clone, body=%wide.region_14.27_spmd.clone.sunk | while | flops 7369006592 | bytes 95885456 | solution.py:118
  1188.3 12.4 while.108
  1200.7 78.6 %custom-call.47 = f32[2,4,128,128]{2,3,1,0:T(8,128)S(1)} custom-call(f32[2,4,128,128]{3,2,1,0:T(8,128)S(1)} %bitcast.769), custom_call_target="InvertDiagBlocksLowerTriangular" | custom-call | tf_op jit(solution)/shard_map/transpose(jvp())/while/body/eval_jaxpr/jit(_solve_triangular)/vmap()/triangular_solve/custom-call.0 | solution.py:96
  1381.0 78.6 %custom-call.47 = f32[2,4,128,128]{2,3,1,0:T(8,128)S(1)} custom-call(f32[2,4,128,128]{3,2,1,0:T(8,128)S(1)} %bitcast.769), custom_call_target="InvertDiagBlocksLowerTriangular" | custom-call | tf_op jit(solution)/shard_map/transpose(jvp())/while/body/eval_jaxpr/jit(_solve_triangular)/vmap()/triangular_solve/custom-call.0 | solution.py:96
  1561.5 78.6 %custom-call.47 = f32[2,4,128,128]{2,3,1,0:T(8,128)S(1)} custom-call(f32[2,4,128,128]{3,2,1,0:T(8,128)S(1)} %bitcast.769), custom_call_target="InvertDiagBlocksLowerTriangular" | custom-call | tf_op jit(solution)/shard_map/transpose(jvp())/while/body/eval_jaxpr/jit(_solve_triangular)/vmap()/triangular_solve/custom-call.0 | solution.py:96
  1742.0 78.6 %custom-call.47 = f32[2,4,128,128]{2,3,1,0:T(8,128)S(1)} custom-call(f32[2,4,128,128]{3,2,1,0:T(8,128)S(1)} %bitcast.769), custom_call_target="InvertDiagBlocksLowerTriangular" | custom-call | tf_op jit(solution)/shard_map/transpose(jvp())/while/body/eval_jaxpr/jit(_solve_triangular)/vmap()/triangular_solve/custom-call.0 | solution.py:96
  2010.0 25.5 %reduce-scatter.32.cloned.1.call-done = bf16[128,256]{1,0:T(8,128)(2,1)} async-done(((bf16[1024,256]{1,0:T(8,128)(2,1)}), bf16[128,256]{1,0:T(8,128)(2,1)}) %reduce-scatter.32.cloned.1.call-update) | async-done | bytes 65552 | tf_op jit(solution)/shard_map/reduce_scatter | solution.py:301
  2037.0 35.9 %reduce-scatter.38.cloned.1.call-done = bf16[128,256]{1,0:T(8,128)(2,1)} async-done(((bf16[1024,256]{1,0:T(8,128)(2,1)}), bf16[128,256]{1,0:T(8,128)(2,1)}) %reduce-scatter.38.cloned.1.call-update) | async-done | bytes 65552 | tf_op jit(solution)/shard_map/reduce_scatter | solution.py:310
  2074.4 37.7 %reduce-scatter.34.cloned.1.call-done = bf16[128,512]{1,0:T(8,128)(2,1)} async-done(((bf16[1024,512]{1,0:T(8,128)(2,1)}), bf16[128,512]{1,0:T(8,128)(2,1)}) %reduce-scatter.34.cloned.1.call-update) | async-done | bytes 131088 | tf_op jit(solution)/shard_map/reduce_scatter | solution.py:304
  2113.7 37.4 %reduce-scatter.36.cloned.1.call-done = bf16[128,512]{1,0:T(8,128)(2,1)} async-done(((bf16[1024,512]{1,0:T(8,128)(2,1)}), bf16[128,512]{1,0:T(8,128)(2,1)}) %reduce-scatter.36.cloned.1.call-update) | async-done | bytes 131088 | tf_op jit(solution)/shard_map/reduce_scatter | solution.py:307
  2152.8 44.6 %reduce-scatter.30.cloned.1.call-done = bf16[256,1024]{1,0:T(8,128)(2,1)} async-done(((bf16[1024,1024]{1,0:T(8,128)(2,1)}), bf16[256,1024]{1,0:T(8,128)(2,1)}) %reduce-scatter.30.cloned.1.call-update) | async-done | bytes 524304 | tf_op jit(solution)/shard_map/reduce_scatter | solution.py:295
  2199.5 43.4 %reduce-scatter.26.cloned.1.call-done = bf16[256,1024]{1,0:T(8,128)(2,1)} async-done(((bf16[1024,1024]{1,0:T(8,128)(2,1)}), bf16[256,1024]{1,0:T(8,128)(2,1)}) %reduce-scatter.26.cloned.1.call-update) | async-done | bytes 524304 | tf_op jit(solution)/shard_map/reduce_scatter | solution.py:248
  2245.9 127.6 %all-reduce.42.cloned.1.call-done = (f32[1024]{0:T(1024)}, f32[4,1024]{1,0:T(4,128)}, f32[4,2048]{1,0:T(4,128)}, f32[4,2048]{1,0:T(4,128)}, f32[8]{0:T(128)}, /*index=5*/f32[128]{0:T(128)}, f32[1024]{0:T(1024)}) async-done(((f32[1024]{0:T(1024)}, f32[4,1024]{1,0:T(4,128)}, f32[4,2048]{1,0:T(4,128)}, f32[4,2048]{1,0:T(4,128)}, f32[8]{0:T(128)}, /*index=5*/f32[128]{0:T(128)}, f32[1024]{0:T(1024)}), ...) | async-done | bytes 90672 | tf_op jit(solution)/shard_map/psum | solution.py:337
  (1239 shorter events, 1004.6 us)
Async XLA Ops:
  7.2 51.0 %all-gather.12.cloned.1.call-start = ((), (), s32[]{:S(2)}) async-start(), calls=%async_computation.14 | async-start | bytes 1179648 | tf_op jit(solution)/shard_map/all_gather | solution.py:194
  8.0 77.7 %all-gather.10.cloned.1.call-start = ((), (), s32[]{:S(2)}) async-start(), calls=%async_computation.13 | async-start | bytes 2621440 | tf_op jit(solution)/shard_map/all_gather | solution.py:212
  11.3 98.5 %all-gather.14.cloned.1.call-start = ((), (), s32[]{:S(2)}) async-start(), calls=%async_computation.15 | async-start | bytes 1179648 | tf_op jit(solution)/shard_map/all_gather | solution.py:195
  12.1 809.8 %reduce-scatter.24.cloned.1.call-start = ((), (), s32[]{:S(2)}) async-start(), calls=%async_computation.16 | async-start | bytes 5242880 | tf_op jit(solution)/shard_map/reduce_scatter | solution.py:233
  744.9 104.6 %all-gather.18.cloned.1.call-start = ((), (), s32[]{:S(2)}) async-start(), calls=%async_computation.18 | async-start | bytes 1622016 | tf_op jit(solution)/shard_map/all_gather | solution.py:199
  745.5 152.1 %all-gather.16.cloned.1.call-start = ((), (), s32[]{:S(2)}) async-start(), calls=%async_computation.17 | async-start | bytes 2621440 | tf_op jit(solution)/shard_map/all_gather | solution.py:242
  823.4 267.3 %copy-start.8 = (f32[256,1024]{1,0:T(8,128)}, f32[256,1024]{1,0:T(8,128)S(1)}, u32[]{:S(2)}) copy-start(f32[256,1024]{1,0:T(8,128)S(1)} %get-tuple-element.2498) | copy-start | bytes 3145732
  823.4 267.3 %copy-start.97 = (f32[256]{0:T(256)}, f32[256]{0:T(256)S(1)}, u32[]{:S(2)}) copy-start(f32[256]{0:T(256)S(1)} %add_rsqrt_fusion.2) | copy-start | bytes 3076
  824.6 99.1 %all-gather.20.cloned.1.call-start = ((), (), s32[]{:S(2)}) async-start(), calls=%async_computation.19 | async-start | bytes 1622016 | tf_op jit(solution)/shard_map/all_gather | solution.py:200
  825.4 125.7 %all-gather.22.cloned.1.call-start = ((), (), s32[]{:S(2)}) async-start(), calls=%async_computation.20 | async-start | bytes 1622016 | tf_op jit(solution)/shard_map/all_gather | solution.py:201
  826.1 172.5 %all-gather.24.cloned.1.call-start = ((), (), s32[]{:S(2)}) async-start(), calls=%async_computation.22 | async-start | bytes 2621440 | tf_op jit(solution)/shard_map/all_gather | solution.py:255
  826.9 261.6 %reduce-scatter.28.cloned.1.call-start = ((), (), s32[]{:S(2)}) async-start(), calls=%async_computation.23 | async-start | bytes 5242880 | tf_op jit(solution)/shard_map/reduce_scatter | solution.py:258
  1012.8 126.3 %all-gather.26.cloned.1.call-start = ((), (), s32[]{:S(2)}) async-start(), calls=%async_computation.24 | async-start | bytes 2621440 | tf_op jit(solution)/shard_map/all_gather | solution.py:286
  1092.5 908.0 %reduce-scatter.46.cloned.1.call-start = ((), (), s32[]{:S(2)}) async-start(), calls=%async_computation.33 | async-start | bytes 1769472
  1100.0 902.4 %reduce-scatter.44.cloned.1.call-start = ((), (), s32[]{:S(2)}) async-start(), calls=%async_computation.32 | async-start | bytes 1769472
  1108.0 896.3 %reduce-scatter.48.cloned.1.call-start = ((), (), s32[]{:S(2)}) async-start(), calls=%async_computation.34 | async-start | bytes 1769472
  1115.6 891.3 %reduce-scatter.40.cloned.1.call-start = ((), (), s32[]{:S(2)}) async-start(), calls=%async_computation.30 | async-start | bytes 294912
  1928.4 80.0 %reduce-scatter.42.cloned.1.call-start = ((), (), s32[]{:S(2)}) async-start(), calls=%async_computation.31 | async-start | bytes 589824
  1933.2 102.3 %reduce-scatter.32.cloned.1.call-start = ((), (), s32[]{:S(2)}) async-start(), calls=%async_computation.26 | async-start | bytes 589824 | tf_op jit(solution)/shard_map/reduce_scatter | solution.py:301
  1939.7 133.2 %reduce-scatter.38.cloned.1.call-start = ((), (), s32[]{:S(2)}) async-start(), calls=%async_computation.29 | async-start | bytes 589824 | tf_op jit(solution)/shard_map/reduce_scatter | solution.py:310
  1958.2 153.9 %reduce-scatter.34.cloned.1.call-start = ((), (), s32[]{:S(2)}) async-start(), calls=%async_computation.27 | async-start | bytes 1179648 | tf_op jit(solution)/shard_map/reduce_scatter | solution.py:304
  1978.2 172.9 %reduce-scatter.36.cloned.1.call-start = ((), (), s32[]{:S(2)}) async-start(), calls=%async_computation.28 | async-start | bytes 1179648 | tf_op jit(solution)/shard_map/reduce_scatter | solution.py:307
  1988.1 209.3 %reduce-scatter.30.cloned.1.call-start = ((), (), s32[]{:S(2)}) async-start(), calls=%async_computation.25 | async-start | bytes 2621440 | tf_op jit(solution)/shard_map/reduce_scatter | solution.py:295
  1995.9 247.1 %reduce-scatter.26.cloned.1.call-start = ((), (), s32[]{:S(2)}) async-start(), calls=%async_computation.21 | async-start | bytes 2621440 | tf_op jit(solution)/shard_map/reduce_scatter | solution.py:248
  2000.4 373.0 %all-reduce.42.cloned.1.call-start = ((), (), s32[]{:S(2)}) async-start(), calls=%async_computation.35 | async-start | bytes 182272 | tf_op jit(solution)/shard_map/psum | solution.py:337
  2001.6 195.8 %copy-start.24 = (bf16[256,1024]{1,0:T(8,128)(2,1)S(1)}, bf16[256,1024]{1,0:T(8,128)(2,1)}, u32[]{:S(2)}) copy-start(bf16[256,1024]{1,0:T(8,128)(2,1)} %param.25) | copy-start | bytes 1572868
  2003.4 239.5 %copy-start.9 = (f32[256,1024]{1,0:T(8,128)S(1)}, f32[256,1024]{1,0:T(8,128)}, u32[]{:S(2)}) copy-start(f32[256,1024]{1,0:T(8,128)} %copy-done.8) | copy-start | bytes 3145732
  2003.5 239.5 %copy-start.26 = (f32[256,1024]{1,0:T(8,128)S(1)}, f32[256,1024]{1,0:T(8,128)}, u32[]{:S(2)}) copy-start(f32[256,1024]{1,0:T(8,128)} %reduce-scatter.28.cloned.1.call-done) | copy-start | bytes 3145732
  2003.5 239.5 %copy-start.38 = (bf16[256,1024]{1,0:T(8,128)(2,1)S(1)}, bf16[256,1024]{1,0:T(8,128)(2,1)}, u32[]{:S(2)}) copy-start(bf16[256,1024]{1,0:T(8,128)(2,1)} %param.26) | copy-start | bytes 1572868
  2003.5 239.5 %copy-start.80 = (f32[1024]{0:T(1024)S(1)}, f32[1024]{0:T(1024)}, u32[]{:S(2)}) copy-start(f32[1024]{0:T(1024)} %param.40) | copy-start | bytes 12292
  2003.5 239.5 %copy-start.98 = (f32[256]{0:T(256)S(1)}, f32[256]{0:T(256)}, u32[]{:S(2)}) copy-start(f32[256]{0:T(256)} %copy-done.97) | copy-start | bytes 3076
  2003.5 239.5 %copy-start.127 = (f32[256]{0:T(256)S(1)}, f32[256]{0:T(256)}, u32[]{:S(2)}) copy-start(f32[256]{0:T(256)} %copy-done.126) | copy-start | bytes 3076
  (210 other events, 5247.1 us)
Sparse Core Ops, SparseCore 0:
  10.0 27.6 all-gather.11
  39.8 45.9 all-gather.9
  87.6 22.1 all-gather.13
  745.0 76.7 reduce-scatter.23
  823.7 25.7 all-gather.17
  851.6 45.9 all-gather.15
  899.6 24.0 all-gather.19
  925.7 25.2 all-gather.21
  952.7 45.9 all-gather.23
  1012.9 75.4 reduce-scatter.27
  1092.6 46.4 all-gather.25
  1142.2 37.1 reduce-scatter.45
  1182.7 38.6 reduce-scatter.43
  1224.5 38.8 reduce-scatter.47
  1928.5 32.4 reduce-scatter.39
  1964.2 34.1 reduce-scatter.41
  2001.4 34.0 reduce-scatter.31
  2038.7 34.1 reduce-scatter.37
  2076.0 36.0 reduce-scatter.33
  2115.1 35.9 reduce-scatter.35
  2153.5 43.8 reduce-scatter.29
  2199.7 43.1 reduce-scatter.25
  2250.5 122.8 all-reduce.41
where the time goes:
time: 2400 us; the launch traced here: 2390 us
  other arithmetic  834 us (35%)
  waiting for transfers between devices  740 us (31%)
  matrix products  419 us (17%)
  local copies, waits for them, and re-layouts  302 us (13%)
  blocking collectives  42.4 us (2%)
  loops' own time  35.1 us (1%)
    another operation x48, other arithmetic, stretch_step(): jax.scipy.linalg.solve_triangular(system, right_side, lower=True, unit_di...  645 us
    psum x1, waiting for transfers between devices, body(): lax.psum((mix_gain_part, mlp_gain_part, back_terms[9], place_cols(conv_qu...  128 us
    reduce_scatter x1, waiting for transfers between devices, body(): lax.psum_scatter(jnp.dot(mixed_low, out_w, preferred_element_type=jnp.flo...  76.3 us
    reduce_scatter x1, waiting for transfers between devices, body(): lax.psum_scatter(dot_cols(gate_grad, gate_w) + dot_cols(up_grad, up_w), '...  75.6 us
    another operation x87, local copies, waits for them, and re-layouts  71.9 us
    dot_general x12, matrix products, stretch_step(): jnp.einsum('hik,hjk->hij', block_query_rows, block_key_rows, precision=EX...  70.7 us
    dot_general x12, matrix products, stretch_step(): jnp.einsum('hij,hjv->hiv', scores, proxy_output, precision=EXACT_PRECISION)  69.7 us
    dot_general x12, matrix products, stretch_step(): jnp.einsum('hik,hjk->hij', block_key_rows, block_key_rows, precision=EXAC...  58 us
  transfers between devices with their start and end apart: 23, of which 17 were waited for; matrix products, arithmetic and copies ran while one was open for 37% of the time, Pallas kernels for 0%

commit v1 on v0

v1 whole, which is shorter than its diff:
```python
from functools import partial

import jax
import jax.numpy as jnp
from jax import lax
from jax.experimental import pallas as pl
from jax.experimental.pallas import tpu as pltpu
from jax.sharding import PartitionSpec as P

HEAD_DIM = 128
EPS = 1e-06
EXACT = lax.Precision.HIGHEST
HIGH = lax.Precision.HIGH
FAST = lax.Precision.DEFAULT
NN = ((1,), (0,))
NT = ((1,), (1,))
TN = ((0,), (0,))
CHUNK = 64
ROWS = 2 * CHUNK


def mm(left, right, dims=NN, precision=HIGH):
    return lax.dot_general(
        left, right, (dims, ((), ())), precision=precision, preferred_element_type=jnp.float32
    )


def softplus(x):
    return jnp.maximum(x, 0.0) + jnp.log1p(jnp.exp(-jnp.abs(x)))


def chunk_masks():
    row = lax.broadcasted_iota(jnp.int32, (ROWS, ROWS), 0)
    col = lax.broadcasted_iota(jnp.int32, (ROWS, ROWS), 1)
    row_tok, col_tok = row & (CHUNK - 1), col & (CHUNK - 1)
    later = row_tok > col_tok
    same_tok = row_tok == col_tok
    pair = same_tok & (row > col)
    levels = []
    size = 1
    while size < CHUNK:
        upper = (row_tok & size) > (col_tok & size)
        together = (row_tok & (-2 * size)) == (col_tok & (-2 * size))
        levels.append(upper & together)
        size *= 2
    return row, col, later | same_tok, later | pair, pair, levels


def invert(lower, ident, pair, levels, precision):
    inverse = ident - jnp.where(pair, lower, 0.0)
    for level in levels:
        step = mm(jnp.where(level, lower, 0.0), inverse, NN, precision)
        inverse = inverse - mm(inverse, step, NN, precision)
    return inverse


def col_sum(x):
    return jnp.sum(x, axis=-1, keepdims=True)


def fwd_kernel(
    heads, per_step, raw_ref, aux_ref, segrow_ref, taps_ref, bias_ref, gain_ref,
    mixed_ref, pre_ref, recall_ref, inv_ref, prox_ref, state_ref, mem_ref, tail_ref, act_ref,
):
    width = HEAD_DIM
    block = per_step * CHUNK
    conv_cols = 5 * heads * width

    @pl.when(pl.program_id(0) == 0)
    def _():
        mem_ref[...] = jnp.zeros_like(mem_ref)
        tail_ref[...] = jnp.zeros_like(tail_ref)

    masks = [aux_ref[:, 2 + s : 3 + s] for s in range(3)]
    for tile in range(5 * heads):
        cols = slice(tile * width, (tile + 1) * width)
        raw = raw_ref[:, cols]
        joined = jnp.concatenate([tail_ref[:, cols], raw], axis=0)
        pre = raw * taps_ref[0:1, cols]
        for s in range(1, 4):
            shifted = pltpu.roll(joined, s, 0)[8:]
            pre = pre + shifted * masks[s - 1] * taps_ref[s : s + 1, cols]
        pre_ref[:, cols] = pre
        tail_ref[:, cols] = raw[block - 8 :]
        act = pre * jax.nn.sigmoid(pre)
        if tile < 3 * heads:
            act = act * lax.rsqrt(col_sum(act * act) + EPS)
        act_ref[:, cols] = act

    row, col, lower_eq, strict, pair, levels = chunk_masks()
    ident = (row == col).astype(jnp.float32)
    tri = (
        lax.broadcasted_iota(jnp.int32, (CHUNK, CHUNK), 0)
        >= lax.broadcasted_iota(jnp.int32, (CHUNK, CHUNK), 1)
    ).astype(jnp.float32)
    rates = raw_ref[:, 6 * heads * width :]
    beta_tile = jax.nn.sigmoid(rates)
    log_tile = -softplus(rates + bias_ref[...])
    units = []
    for part in range(per_step):
        rows = slice(part * CHUNK, (part + 1) * CHUNK)
        cumul = mm(tri, log_tile[rows], NN, EXACT)
        cumul_t = jnp.concatenate([cumul, cumul], axis=0).T
        aux = aux_ref[rows]
        aux2 = jnp.concatenate([aux, aux], axis=0)
        same = (aux2[:, 8:9] == segrow_ref[part]) & lower_eq
        end = cumul[CHUNK - 1 :]
        for head in range(heads):
            key1 = act_ref[rows, (heads + 2 * head) * width : (heads + 2 * head + 1) * width]
            key2 = act_ref[rows, (heads + 2 * head + 1) * width : (heads + 2 * head + 2) * width]
            val1 = act_ref[rows, (3 * heads + 2 * head) * width : (3 * heads + 2 * head + 1) * width]
            val2 = act_ref[rows, (3 * heads + 2 * head + 1) * width : (3 * heads + 2 * head + 2) * width]
            query = act_ref[rows, head * width : (head + 1) * width]
            keys = jnp.concatenate([key1, key2], axis=0)
            lane = 3 * head
            c_tok = cumul[:, lane + 2 : lane + 3]
            c_end = end[:, lane + 2 : lane + 3]
            c_col = jnp.concatenate([c_tok, c_tok], axis=0)
            c_row = cumul_t[lane + 2 : lane + 3, :]
            decay = jnp.where(same, jnp.exp(jnp.minimum(c_col - c_row, 0.0)), 0.0)
            beta1 = beta_tile[rows, lane : lane + 1]
            beta2 = beta_tile[rows, lane + 1 : lane + 2]
            beta = jnp.concatenate([beta1, beta2], axis=0)
            start = aux[:, 0:1] * jnp.exp(c_tok)
            start2 = jnp.concatenate([start, start], axis=0)
            final = aux[:, 1:2] * jnp.exp(c_end - c_tok)
            final2 = jnp.concatenate([final, final], axis=0)
            total = aux[CHUNK - 1 :, 0:1] * jnp.exp(c_end)
            dots = mm(jnp.concatenate([keys, query], axis=0), keys, NT)
            lower = jnp.where(strict, beta * decay * dots[:ROWS], 0.0)
            scores = decay[CHUNK:] * dots[ROWS:]
            inverse = invert(lower, ident, pair, levels, HIGH)
            inv_ref[part * heads + head] = inverse
            values = jnp.concatenate([val1, val2], axis=0)
            solved = mm(
                inverse, jnp.concatenate([beta * values, beta * start2 * keys], axis=1)
            )
            probe = jnp.concatenate([solved[:, width:], start * query], axis=0)
            units.append(
                (part, head, rows, probe, solved[:, :width], scores, total, final2 * keys)
            )
    for part, head, rows, probe, base, scores, total, final_keys in units:
        memory = mem_ref[head]
        state_ref[part * heads + head] = memory
        seen = mm(probe, memory)
        proxy = base - seen[:ROWS]
        prox_ref[part * heads + head] = proxy
        mem_ref[head] = total * memory + mm(final_keys, proxy, TN)
        recall = seen[ROWS:] + mm(scores, proxy)
        cols = slice(head * width, (head + 1) * width)
        recall_ref[rows, cols] = recall
        scale = lax.rsqrt(jnp.mean(recall * recall, axis=-1, keepdims=True) + EPS)
        gate = raw_ref[rows, (5 * heads + head) * width : (5 * heads + head + 1) * width]
        mixed = recall * scale * gain_ref[...] * (gate * jax.nn.sigmoid(gate))
        mixed_ref[rows, cols] = mixed.astype(jnp.bfloat16)


def bwd_kernel(
    heads, per_step, grad_ref, raw_ref, aux_ref, segrow_ref, pre_ref, recall_ref, inv_ref,
    prox_ref, state_ref, taps_ref, bias_ref, gain_ref,
    low_ref, taps_grad_ref, bias_grad_ref, gain_grad_ref, adj_ref, head_ref, act_ref, norm_ref, dact_ref,
):
    width = HEAD_DIM
    block = per_step * CHUNK

    @pl.when(pl.program_id(0) == 0)
    def _():
        adj_ref[...] = jnp.zeros_like(adj_ref)
        head_ref[...] = jnp.zeros_like(head_ref)
        taps_grad_ref[...] = jnp.zeros_like(taps_grad_ref)
        bias_grad_ref[...] = jnp.zeros_like(bias_grad_ref)
        gain_grad_ref[...] = jnp.zeros_like(gain_grad_ref)

    for tile in range(5 * heads):
        cols = slice(tile * width, (tile + 1) * width)
        pre = pre_ref[:, cols]
        act = pre * jax.nn.sigmoid(pre)
        if tile < 3 * heads:
            scale = lax.rsqrt(col_sum(act * act) + EPS)
            norm_ref[:, cols] = jnp.broadcast_to(scale, act.shape)
            act = act * scale
        act_ref[:, cols] = act

    row, col, lower_eq, strict, pair, levels = chunk_masks()
    tri_t = (
        lax.broadcasted_iota(jnp.int32, (CHUNK, CHUNK), 0)
        <= lax.broadcasted_iota(jnp.int32, (CHUNK, CHUNK), 1)
    ).astype(jnp.float32)
    tri = (
        lax.broadcasted_iota(jnp.int32, (CHUNK, CHUNK), 0)
        >= lax.broadcasted_iota(jnp.int32, (CHUNK, CHUNK), 1)
    ).astype(jnp.float32)
    lanes = lax.broadcasted_iota(jnp.int32, (CHUNK, width), 1)
    rates = raw_ref[:, 6 * heads * width :]
    beta_tile = jax.nn.sigmoid(rates)
    keep_in = rates + bias_ref[...]
    log_tile = -softplus(keep_in)
    gain_total = jnp.zeros((1, width), jnp.float32)
    bias_total = jnp.zeros((1, width), jnp.float32)
    for part in reversed(range(per_step)):
        rows = slice(part * CHUNK, (part + 1) * CHUNK)
        cumul = mm(tri, log_tile[rows], NN, EXACT)
        cumul_t = jnp.concatenate([cumul, cumul], axis=0).T
        aux = aux_ref[rows]
        aux2 = jnp.concatenate([aux, aux], axis=0)
        same = (aux2[:, 8:9] == segrow_ref[part]) & lower_eq
        end = cumul[CHUNK - 1 :]
        beta_grad = jnp.zeros((CHUNK, width), jnp.float32)
        cumul_grad = jnp.zeros((CHUNK, width), jnp.float32)
        end_grad = jnp.zeros((CHUNK, width), jnp.float32)
        for head in range(heads):
            spot = part * heads + head
            k1 = slice((heads + 2 * head) * width, (heads + 2 * head + 1) * width)
            k2 = slice((heads + 2 * head + 1) * width, (heads + 2 * head + 2) * width)
            v1 = slice((3 * heads + 2 * head) * width, (3 * heads + 2 * head + 1) * width)
            v2 = slice((3 * heads + 2 * head + 1) * width, (3 * heads + 2 * head + 2) * width)
            q0 = slice(head * width, (head + 1) * width)
            g0 = slice((5 * heads + head) * width, (5 * heads + head + 1) * width)
            keys = jnp.concatenate([act_ref[rows, k1], act_ref[rows, k2]], axis=0)
            values = jnp.concatenate([act_ref[rows, v1], act_ref[rows, v2]], axis=0)
            query = act_ref[rows, q0]
            recall = recall_ref[rows, q0]
            grad = grad_ref[rows, q0]
            gate = raw_ref[rows, g0]
            gate_sig = jax.nn.sigmoid(gate)
            silu_gate = gate * gate_sig
            scale = lax.rsqrt(jnp.mean(recall * recall, axis=-1, keepdims=True) + EPS)
            normed = recall * scale
            gain_total = gain_total + jnp.sum(grad * normed * silu_gate, axis=0, keepdims=True)
            weighted = grad * gain_ref[...]
            low_ref[rows, g0] = (
                weighted * normed * gate_sig * (1.0 + gate * (1.0 - gate_sig))
            ).astype(jnp.bfloat16)
            normed_grad = weighted * silu_gate
            out_grad = scale * (
                normed_grad - normed * jnp.mean(normed_grad * normed, axis=-1, keepdims=True)
            )
            lane = 3 * head
            c_tok = cumul[:, lane + 2 : lane + 3]
            c_end = end[:, lane + 2 : lane + 3]
            c_col = jnp.concatenate([c_tok, c_tok], axis=0)
            c_row = cumul_t[lane + 2 : lane + 3, :]
            decay = jnp.where(same, jnp.exp(jnp.minimum(c_col - c_row, 0.0)), 0.0)
            beta = jnp.concatenate(
                [beta_tile[rows, lane : lane + 1], beta_tile[rows, lane + 1 : lane + 2]], axis=0
            )
            start = aux[:, 0:1] * jnp.exp(c_tok)
            start2 = jnp.concatenate([start, start], axis=0)
            final = aux[:, 1:2] * jnp.exp(c_end - c_tok)
            final2 = jnp.concatenate([final, final], axis=0)
            total = aux[CHUNK - 1 :, 0:1] * jnp.exp(c_end)
            dots = mm(jnp.concatenate([keys, query], axis=0), keys, NT)
            key_decay = jnp.where(strict, decay * dots[:ROWS], 0.0)
            scores = decay[CHUNK:] * dots[ROWS:]
            adjoint = adj_ref[head]
            memory = state_ref[spot]
            proxy = prox_ref[spot]
            proxy_grad = mm(scores, out_grad, TN) + mm(final2 * keys, adjoint)
            right_grad = mm(inv_ref[spot], proxy_grad, TN)
            both_grad = jnp.concatenate([right_grad, out_grad], axis=0)
            beta_start = beta * start2
            adj_ref[head] = total * adjoint + mm(
                jnp.concatenate([-beta_start * keys, start * query], axis=0), both_grad, TN
            )
            outer = mm(both_grad, proxy, NT)
            through = mm(both_grad, memory, NT)
            final_part = final2 * mm(proxy, adjoint, NT)
            lower_grad = -outer[:ROWS]
            beta_part = lower_grad * key_decay
            dots_grad = jnp.where(strict, lower_grad * beta * decay, 0.0)
            score_grad = outer[ROWS:] * decay[CHUNK:]
            log_part = beta_part * beta
            log_part = jnp.concatenate(
                [log_part[:CHUNK], log_part[CHUNK:] + outer[ROWS:] * scores], axis=0
            )
            inner = mm(
                jnp.concatenate([dots_grad + dots_grad.T, score_grad], axis=0), keys
            )
            key_through = col_sum(keys * through[:ROWS])
            query_through = start * col_sum(query * through[ROWS:])
            final_sum = col_sum(keys * final_part)
            key_grad = (
                inner[:ROWS]
                + mm(score_grad, query, TN)
                - beta_start * through[:ROWS]
                + final_part
            )
            query_grad = inner[ROWS:] + start * through[ROWS:]
            value_grad = beta * right_grad
            beta_col = (
                col_sum(right_grad * values) - start2 * key_through + col_sum(beta_part)
            )
            c_grad = col_sum(log_part - log_part.T) - beta_start * key_through - final_sum
            c_grad = c_grad[:CHUNK] + c_grad[CHUNK:] + query_through
            end_part = jnp.sum(final_sum, axis=0, keepdims=True) + total * jnp.sum(
                col_sum(memory * adjoint), axis=0, keepdims=True
            )
            beta_grad = jnp.where(lanes == lane, beta_col[:CHUNK], beta_grad)
            beta_grad = jnp.where(lanes == lane + 1, beta_col[CHUNK:], beta_grad)
            cumul_grad = jnp.where(lanes == lane + 2, c_grad, cumul_grad)
            end_grad = jnp.where(lanes == lane + 2, end_part, end_grad)
            dact_ref[rows, k1] = key_grad[:CHUNK]
            dact_ref[rows, k2] = key_grad[CHUNK:]
            dact_ref[rows, v1] = value_grad[:CHUNK]
            dact_ref[rows, v2] = value_grad[CHUNK:]
            dact_ref[rows, q0] = query_grad
        log_grad = mm(tri_t, cumul_grad, NN, EXACT) + end_grad
        keep_sig = jax.nn.sigmoid(keep_in[rows])
        beta_rows = beta_tile[rows]
        keep_grad = -log_grad * keep_sig * aux[:, 2:3]
        rate_grad = beta_grad * beta_rows * (1.0 - beta_rows) + keep_grad
        bias_total = bias_total + jnp.sum(keep_grad, axis=0, keepdims=True)
        low_ref[rows, 6 * heads * width :] = rate_grad.astype(jnp.bfloat16)
    gain_grad_ref[...] += gain_total
    bias_grad_ref[...] += bias_total

    masks = [aux_ref[:, 5 + s : 6 + s] for s in range(3)]
    for tile in range(5 * heads):
        cols = slice(tile * width, (tile + 1) * width)
        pre = pre_ref[:, cols]
        sig = jax.nn.sigmoid(pre)
        grad = dact_ref[:, cols]
        if tile < 3 * heads:
            act = act_ref[:, cols]
            grad = norm_ref[:, cols] * (grad - act * col_sum(grad * act))
        grad = grad * sig * (1.0 + pre * (1.0 - sig))
        raw = raw_ref[:, cols]
        joined = jnp.concatenate([grad, head_ref[:, cols]], axis=0)
        head_ref[:, cols] = grad[:8]
        raw_grad = grad * taps_ref[0:1, cols]
        taps_grad_ref[0:1, cols] += jnp.sum(raw * grad, axis=0, keepdims=True)
        for s in range(1, 4):
            shifted = pltpu.roll(joined, block + 8 - s, 0)[:block] * masks[s - 1]
            raw_grad = raw_grad + shifted * taps_ref[s : s + 1, cols]
            taps_grad_ref[s : s + 1, cols] += jnp.sum(raw * shifted, axis=0, keepdims=True)
        low_ref[:, cols] = raw_grad.astype(jnp.bfloat16)


def token_aux(segments):
    length = segments.shape[0]
    seg = segments.astype(jnp.int32)
    chunks = seg.reshape(length // CHUNK, CHUNK)
    last = chunks[:, -1]
    before = jnp.concatenate([jnp.full((1,), -1, jnp.int32), last[:-1]])
    columns = [
        (chunks == before[:, None]).reshape(length),
        (chunks == last[:, None]).reshape(length),
    ]
    for s in range(1, 4):
        columns.append(jnp.pad(seg, (s, 0), constant_values=-1)[:length] == seg)
    for s in range(1, 4):
        columns.append(jnp.pad(seg, (0, s), constant_values=-1)[s:] == seg)
    columns.append(seg)
    columns += [jnp.zeros_like(seg)] * 7
    aux = jnp.stack([c.astype(jnp.float32) for c in columns], axis=1)
    row = chunks.astype(jnp.float32)
    return aux, jnp.concatenate([row, row], axis=1)[:, None, :]


def mixer_forward(raw, aux, segrow, taps, bias, gain, heads, per_step):
    length = raw.shape[0]
    width = HEAD_DIM
    block = per_step * CHUNK
    steps = length // block
    units = per_step * heads
    total_units = steps * units
    cols = raw.shape[1]
    f32 = jnp.float32
    tiles = lambda i: (i, 0)
    cubes = lambda i: (i, 0, 0)
    fixed = lambda i: (0, 0)
    unit_spec = pl.BlockSpec((units, ROWS, width), cubes)
    unit_shape = jax.ShapeDtypeStruct((total_units, ROWS, width), f32)
    return pl.pallas_call(
        partial(fwd_kernel, heads, per_step),
        grid=(steps,),
        in_specs=[
            pl.BlockSpec((block, cols), tiles),
            pl.BlockSpec((block, 16), tiles),
            pl.BlockSpec((per_step, 1, ROWS), cubes),
            pl.BlockSpec(taps.shape, fixed),
            pl.BlockSpec((1, width), fixed),
            pl.BlockSpec((1, width), fixed),
        ],
        out_specs=[
            pl.BlockSpec((block, heads * width), tiles),
            pl.BlockSpec((block, 5 * heads * width), tiles),
            pl.BlockSpec((block, heads * width), tiles),
            unit_spec,
            unit_spec,
            unit_spec,
        ],
        out_shape=[
            jax.ShapeDtypeStruct((length, heads * width), jnp.bfloat16),
            jax.ShapeDtypeStruct((length, 5 * heads * width), f32),
            jax.ShapeDtypeStruct((length, heads * width), f32),
            unit_shape,
            unit_shape,
            unit_shape,
        ],
        scratch_shapes=[
            pltpu.VMEM((heads, width, width), f32),
            pltpu.VMEM((8, 5 * heads * width), f32),
            pltpu.VMEM((block, 5 * heads * width), f32),
        ],
        compiler_params=pltpu.CompilerParams(
            dimension_semantics=("arbitrary",), vmem_limit_bytes=48 * 1024 * 1024
        ),
        name="mixer_forward",
    )(raw, aux, segrow, taps, bias, gain)


def mixer_backward(grad, raw, aux, segrow, saved, taps, bias, gain, heads, per_step):
    pre, recall, inverse, proxy, state = saved
    length = raw.shape[0]
    width = HEAD_DIM
    block = per_step * CHUNK
    steps = length // block
    units = per_step * heads
    cols = raw.shape[1]
    f32 = jnp.float32
    tiles = lambda i: (steps - 1 - i, 0)
    cubes = lambda i: (steps - 1 - i, 0, 0)
    fixed = lambda i: (0, 0)
    unit_spec = pl.BlockSpec((units, ROWS, width), cubes)
    return pl.pallas_call(
        partial(bwd_kernel, heads, per_step),
        grid=(steps,),
        in_specs=[
            pl.BlockSpec((block, heads * width), tiles),
            pl.BlockSpec((block, cols), tiles),
            pl.BlockSpec((block, 16), tiles),
            pl.BlockSpec((per_step, 1, ROWS), cubes),
            pl.BlockSpec((block, 5 * heads * width), tiles),
            pl.BlockSpec((block, heads * width), tiles),
            unit_spec,
            unit_spec,
            unit_spec,
            pl.BlockSpec(taps.shape, fixed),
            pl.BlockSpec((1, width), fixed),
            pl.BlockSpec((1, width), fixed),
        ],
        out_specs=[
            pl.BlockSpec((block, cols), tiles),
            pl.BlockSpec(taps.shape, fixed),
            pl.BlockSpec((1, width), fixed),
            pl.BlockSpec((1, width), fixed),
        ],
        out_shape=[
            jax.ShapeDtypeStruct((length, cols), jnp.bfloat16),
            jax.ShapeDtypeStruct(taps.shape, f32),
            jax.ShapeDtypeStruct((1, width), f32),
            jax.ShapeDtypeStruct((1, width), f32),
        ],
        scratch_shapes=[
            pltpu.VMEM((heads, width, width), f32),
            pltpu.VMEM((8, 5 * heads * width), f32),
            pltpu.VMEM((block, 5 * heads * width), f32),
            pltpu.VMEM((block, 3 * heads * width), f32),
            pltpu.VMEM((block, 5 * heads * width), f32),
        ],
        compiler_params=pltpu.CompilerParams(
            dimension_semantics=("arbitrary",), vmem_limit_bytes=48 * 1024 * 1024
        ),
        name="mixer_backward",
    )(grad, raw, aux, segrow, pre, recall, inverse, proxy, state, taps, bias, gain)


def dot_rows(left, right):
    return lax.dot_general(
        left, right, (((0,), (0,)), ((), ())), preferred_element_type=jnp.float32
    )


def dot_cols(left, right):
    return lax.dot_general(
        left, right, (((1,), (1,)), ((), ())), preferred_element_type=jnp.float32
    )


def row_norm(values, gain):
    scale = lax.rsqrt(jnp.mean(values * values, axis=-1, keepdims=True) + EPS)
    return (values * scale * gain, scale)


def norm_back(grad, values, scale, gain):
    normed = values * scale
    gain_grad = jnp.sum(grad * normed, axis=0)
    weighted = grad * gain
    value_grad = scale * (weighted - normed * jnp.mean(weighted * normed, axis=-1, keepdims=True))
    return (value_grad, gain_grad)


def swiglu_back(hidden_grad, gate_pre, up_pre):
    gate_sigmoid = jax.nn.sigmoid(gate_pre)
    gate_grad = hidden_grad * up_pre * gate_sigmoid * (1.0 + gate_pre * (1.0 - gate_sigmoid))
    up_grad = hidden_grad * gate_pre * gate_sigmoid
    return (gate_grad.astype(jnp.bfloat16), up_grad.astype(jnp.bfloat16))


def body(
    layer_input,
    cotangent,
    segments,
    mix_gain,
    query_weight,
    key_weight,
    value_weight,
    outgate_weight,
    rate_weight,
    conv_query,
    conv_key,
    conv_value,
    decay_bias,
    out_gain,
    out_weight,
    mlp_gain,
    gate_weight,
    up_weight,
    down_weight,
):
    head_index = lax.axis_index("head")
    local_rows = layer_input.shape[0]
    local_heads = query_weight.shape[1] // HEAD_DIM
    own_weight = jnp.concatenate(
        [
            query_weight,
            key_weight,
            value_weight,
            outgate_weight,
            jnp.pad(rate_weight, ((0, 0), (0, HEAD_DIM - rate_weight.shape[1]))),
        ],
        axis=1,
    )
    proj_w, out_w, gate_w, up_w, down_w = (
        lax.all_gather(own_weight, "batch", axis=0, tiled=True),
        lax.all_gather(out_weight, "batch", axis=1, tiled=True),
        lax.all_gather(gate_weight, "batch", axis=0, tiled=True),
        lax.all_gather(up_weight, "batch", axis=0, tiled=True),
        lax.all_gather(down_weight, "batch", axis=1, tiled=True),
    )
    def head_cols(table, per_head):
        return lax.dynamic_slice_in_dim(
            table, head_index * local_heads * per_head, local_heads * per_head, axis=table.ndim - 1
        )

    resid_in = layer_input.astype(jnp.float32)
    normed_in, scale_in = row_norm(resid_in, mix_gain)
    rows_in = lax.all_gather(normed_in.astype(jnp.bfloat16), "head", axis=0, tiled=True)
    raw = jnp.dot(rows_in, proj_w, preferred_element_type=jnp.float32)
    taps = jnp.concatenate(
        [
            head_cols(conv_query, HEAD_DIM),
            head_cols(conv_key, 2 * HEAD_DIM),
            head_cols(conv_value, 2 * HEAD_DIM),
        ],
        axis=1,
    )
    own_bias = head_cols(decay_bias, 1)
    bias = jnp.stack([jnp.zeros_like(own_bias), jnp.zeros_like(own_bias), own_bias], axis=1)
    bias = jnp.pad(bias.reshape(-1), (0, HEAD_DIM - 3 * local_heads))[None]
    aux, segrow = token_aux(segments)
    gain = out_gain[None]
    per_step = 2
    mixed_low, *saved = mixer_forward(raw, aux, segrow, taps, bias, gain, local_heads, per_step)
    resid_mid = resid_in + lax.psum_scatter(
        jnp.dot(mixed_low, out_w, preferred_element_type=jnp.float32),
        "head",
        scatter_dimension=0,
        tiled=True,
    )
    normed_mid, scale_mid = row_norm(resid_mid, mlp_gain)
    normed_mid_low = normed_mid.astype(jnp.bfloat16)
    grad_out = cotangent.astype(jnp.float32)
    rows_mid = lax.all_gather(normed_mid_low, "head", axis=0, tiled=True)
    gate_pre = jnp.dot(rows_mid, gate_w, preferred_element_type=jnp.float32)
    up_pre = jnp.dot(rows_mid, up_w, preferred_element_type=jnp.float32)
    hidden = (jax.nn.silu(gate_pre) * up_pre).astype(jnp.bfloat16)
    layer_output = (
        resid_mid
        + lax.psum_scatter(
            jnp.dot(hidden, down_w, preferred_element_type=jnp.float32).astype(jnp.bfloat16),
            "head",
            scatter_dimension=0,
            tiled=True,
        ).astype(jnp.float32)
    ).astype(jnp.bfloat16)
    rows_grad = lax.all_gather(cotangent, "head", axis=0, tiled=True)
    hidden_grad = dot_cols(rows_grad, down_w)
    gate_grad, up_grad = swiglu_back(hidden_grad, gate_pre, up_pre)
    mid_grad = lax.psum_scatter(
        dot_cols(gate_grad, gate_w) + dot_cols(up_grad, up_w),
        "head",
        scatter_dimension=0,
        tiled=True,
    )
    gate_total, up_total, down_total = (
        lax.psum_scatter(
            dot_rows(rows_mid, gate_grad).astype(jnp.bfloat16),
            "batch",
            scatter_dimension=0,
            tiled=True,
        ).astype(jnp.float32),
        lax.psum_scatter(
            dot_rows(rows_mid, up_grad).astype(jnp.bfloat16),
            "batch",
            scatter_dimension=0,
            tiled=True,
        ).astype(jnp.float32),
        lax.psum_scatter(
            dot_rows(hidden, rows_grad).astype(jnp.bfloat16),
            "batch",
            scatter_dimension=1,
            tiled=True,
        ).astype(jnp.float32),
    )
    mid_back, mlp_gain_part = norm_back(mid_grad, resid_mid, scale_mid, mlp_gain)
    resid_grad = grad_out + mid_back
    rows_resid_grad = lax.all_gather(resid_grad.astype(jnp.bfloat16), "head", axis=0, tiled=True)
    mixed_grad = dot_cols(rows_resid_grad, out_w)
    out_sum = dot_rows(mixed_low, rows_resid_grad)
    raw_low, taps_grad, bias_grad, gain_grad = mixer_backward(
        mixed_grad, raw, aux, segrow, saved, taps, bias, gain, local_heads, per_step
    )
    proj_sum = dot_rows(rows_in, raw_low)
    total = dot_cols(raw_low, proj_w)
    in_grad = lax.psum_scatter(
        total.astype(jnp.bfloat16), "head", scatter_dimension=0, tiled=True
    ).astype(jnp.float32)
    in_back, mix_gain_part = norm_back(in_grad, resid_in, scale_in, mix_gain)
    input_grad = resid_grad + in_back
    proj_total, out_total = (
        lax.psum_scatter(
            proj_sum.astype(jnp.bfloat16), "batch", scatter_dimension=0, tiled=True
        ).astype(jnp.float32),
        lax.psum_scatter(
            out_sum.astype(jnp.bfloat16), "batch", scatter_dimension=1, tiled=True
        ).astype(jnp.float32),
    )
    unit = local_heads * HEAD_DIM
    query_sum = proj_total[:, :unit]
    key_sum = proj_total[:, unit : 3 * unit]
    value_sum = proj_total[:, 3 * unit : 5 * unit]
    outgate_sum = proj_total[:, 5 * unit : 6 * unit]
    rate_sum = proj_total[:, 6 * unit : 6 * unit + 3 * local_heads]
    own_bias_grad = bias_grad[0, : 3 * local_heads].reshape(local_heads, 3)[:, 2]

    def place_cols(table_shape, local_part, per_head):
        return lax.dynamic_update_slice_in_dim(
            jnp.zeros(table_shape, jnp.float32),
            local_part,
            head_index * local_heads * per_head,
            axis=len(table_shape) - 1,
        )

    (
        mix_gain_grad,
        mlp_gain_grad,
        out_gain_grad,
        conv_query_grad,
        conv_key_grad,
        conv_value_grad,
        decay_bias_grad,
    ) = lax.psum(
        (
            mix_gain_part,
            mlp_gain_part,
            gain_grad[0],
            place_cols(conv_query.shape, taps_grad[:, :unit], HEAD_DIM),
            place_cols(conv_key.shape, taps_grad[:, unit : 3 * unit], 2 * HEAD_DIM),
            place_cols(conv_value.shape, taps_grad[:, 3 * unit :], 2 * HEAD_DIM),
            place_cols(decay_bias.shape, own_bias_grad, 1),
        ),
        ("head", "batch"),
    )
    return (
        layer_output,
        input_grad,
        mix_gain_grad,
        query_sum,
        key_sum,
        value_sum,
        outgate_sum,
        rate_sum,
        conv_query_grad,
        conv_key_grad,
        conv_value_grad,
        decay_bias_grad,
        out_gain_grad,
        out_total,
        mlp_gain_grad,
        gate_total,
        up_total,
        down_total,
    )


def solution(mesh):
    placed = (
        P(("batch", "head"), None),
        P(("batch", "head"), None),
        P("batch"),
        P(),
        P("batch", "head"),
        P("batch", "head"),
        P("batch", "head"),
        P("batch", "head"),
        P("batch", "head"),
        P(),
        P(),
        P(),
        P(),
        P(),
        P("head", "batch"),
        P(),
        P("batch", "head"),
        P("batch", "head"),
        P("head", "batch"),
    )
    return jax.shard_map(
        body,
        mesh=mesh,
        in_specs=placed,
        out_specs=(
            P(("batch", "head"), None),
            P(("batch", "head"), None),
            P(),
            P("batch", "head"),
            P("batch", "head"),
            P("batch", "head"),
            P("batch", "head"),
            P("batch", "head"),
            P(),
            P(),
            P(),
            P(),
            P(),
            P("head", "batch"),
            P(),
            P("batch", "head"),
            P("batch", "head"),
            P("head", "batch"),
        ),
        check_vma=False,
    )
```

time: 2400 us -> 1040 us (0.43)
  other arithmetic: 834 us -> 19 us
  matrix products: 419 us -> 74.2 us
  local copies, waits for them, and re-layouts: 302 us -> 36.8 us
  Pallas kernels: 0 us -> 134 us
  loops' own time: 35.1 us -> 0 us
  blocking collectives: 42.4 us -> 12.5 us
    another operation x93 -> x1, other arithmetic: 662 us -> 0.08 us  [token_aux(): aux = jnp.stack([c.astype(jnp.float32) for c in columns], axis=1)]
    dot_general x81 -> x1, matrix products: 300 us -> 9.43 us  [body(): raw = jnp.dot(rows_in, proj_w, preferred_element_type=jnp.float32)]
    pallas_call x0 -> x2, Pallas kernels: none -> 134 us  [the longest x1 82.7 us: mixer_forward(): pl.pallas_call(partial(fwd_kernel, heads, per_step), grid=(steps,), in_sp...]
    another operation x175 -> x11, local copies, waits for them, and re-layouts: 121 us -> 0.57 us  [the longest x5 0.31 us: token_aux(): aux = jnp.stack([c.astype(jnp.float32) for c in columns], axis=1)]
    reduce_scatter x4 -> x1, waiting for transfers between devices: 137 us -> 47.6 us  [body(): lax.psum_scatter(proj_sum.astype(jnp.bfloat16), 'batch', scatter_dimensio...]
    unnamed x28 -> x22, waiting for transfers between devices: 4.29 us -> 77 us
    reduce_sum x25 -> x0, other arithmetic: 51.7 us -> none  [the longest x2 16.3 us: short_conv(): jnp.where((earlier == segments)[:, None], shifted, 0.0) * taps[offset]]
    another operation x56 -> x0, matrix products: 51 us -> none  [stretch_step(): jax.scipy.linalg.solve_triangular(system, right_side, lower=True, unit_di...]
  transfers between devices with their start and end apart: 23 -> 18, of which waited for: 17 -> 16; matrix products, arithmetic and copies ran while one was open for 37% -> 8% of each run, Pallas kernels for 0% -> 5%
where the time goes in v1:
time: 1040 us; the launch traced here: 1030 us
  waiting for transfers between devices  742 us (71%)
  Pallas kernels  134 us (13%)
  matrix products  74.2 us (7%)
  local copies, waits for them, and re-layouts  36.8 us (4%)
  other arithmetic  19 us (2%)
  between operations  15.3 us (1%)
  blocking collectives  12.5 us (1%)
    psum x1, waiting for transfers between devices, body(): lax.psum((mix_gain_part, mlp_gain_part, gain_grad[0], place_cols(conv_que...  126 us
    pallas_call x1, Pallas kernels, mixer_forward(): pl.pallas_call(partial(fwd_kernel, heads, per_step), grid=(steps,), in_sp...  82.7 us
    unnamed x22, waiting for transfers between devices  77 us
    reduce_scatter x1, waiting for transfers between devices, body(): lax.psum_scatter(jnp.dot(mixed_low, out_w, preferred_element_type=jnp.flo...  76.3 us
    reduce_scatter x1, waiting for transfers between devices, body(): lax.psum_scatter(dot_cols(gate_grad, gate_w) + dot_cols(up_grad, up_w), '...  75.6 us
    pallas_call x1, Pallas kernels, mixer_backward(): pl.pallas_call(partial(bwd_kernel, heads, per_step), grid=(steps,), in_sp...  51.4 us
    all_gather x1, waiting for transfers between devices, body(): rows_mid = lax.all_gather(normed_mid_low, 'head', axis=0, tiled=True)  48 us
    all_gather x1, waiting for transfers between devices, body(): rows_grad = lax.all_gather(cotangent, 'head', axis=0, tiled=True)  47.6 us
  transfers between devices with their start and end apart: 18, of which 16 were waited for; matrix products, arithmetic and copies ran while one was open for 8% of the time, Pallas kernels for 5%

profile of v1, /device:TPU:0, one launch (start us, length us, event | category | flops | bytes accessed | tf_op | source)
XLA Modules:
  0.0 1035.0 jit_solution(5803169925435822698)
XLA Ops:
  14.3 12.5 %all_gather.29 = bf16[256,1024]{1,0:T(8,128)(2,1)} all-gather(bf16[256,128]{1,0:T(8,128)(2,1)S(1)} %copy-done.19), channel_id=1, replica_groups=mesh['head'=4,'batch'=8] {'batch'}, dimensions={1}, use_global_device_ids=true | all-gather | bytes 589824 | tf_op jit(solution)/shard_map/all_gather | solution.py:537
  26.8 32.7 %all-gather.9.cloned.1.call-done = bf16[1024,1024]{1,0:T(8,128)(2,1)} async-done(((bf16[256,1024]{1,0:T(8,128)(2,1)}), bf16[1024,1024]{1,0:T(8,128)(2,1)}) %all-gather.9.cloned.1.call-update) | async-done | bytes 2097168 | tf_op jit(solution)/shard_map/all_gather | solution.py:549
  59.5 34.6 %all-gather.11.cloned.1.call-done = bf16[1024,1664]{1,0:T(8,128)(2,1)} async-done(((bf16[128,1664]{1,0:T(8,128)(2,1)}), bf16[1024,1664]{1,0:T(8,128)(2,1)}) %all-gather.11.cloned.1.call-update) | async-done | bytes 3407888 | tf_op jit(solution)/shard_map/all_gather | solution.py:536
  94.2 9.4 fusion.26.raw_ref
  103.6 82.7 %mixer_forward.1 = (bf16[1024,256]{1,0:T(8,128)(2,1)S(1)}, f32[1024,1280]{1,0:T(8,128)}, f32[1024,256]{1,0:T(8,128)S(1)}, f32[32,128,128]{2,1,0:T(8,128)S(1)}, f...) custom-call(f32[1024,1664]{1,0:T(8,128)} %fusion.26.raw_ref, f32[1024,16]{1,0:T(8,128)S(1)} %copy.54.aux_ref, ...), custom_call_target="tpu_custom_call" | custom-call | tf_op jit(solution)/shard_map/mixer_forward/pallas_call | solution.py:374
  190.7 76.3 %reduce-scatter.18.cloned.1.call-done = f32[256,1024]{1,0:T(8,128)} async-done(((f32[1024,1024]{1,0:T(8,128)}), f32[256,1024]{1,0:T(8,128)}) %reduce-scatter.18.cloned.1.call-update) | async-done | bytes 1048592 | tf_op jit(solution)/shard_map/reduce_scatter | solution.py:566
  272.8 21.9 %all-gather.15.cloned.1.call-done = bf16[1024,704]{0,1:T(8,128)(2,1)} async-done(((bf16[128,704]{0,1:T(8,128)(2,1)}), bf16[1024,704]{0,1:T(8,128)(2,1)}) %all-gather.15.cloned.1.call-update) | async-done | bytes 1441808 | tf_op jit(solution)/shard_map/all_gather | solution.py:538
  294.7 48.0 %all-gather.13.cloned.1.call-done = bf16[1024,1024]{1,0:T(8,128)(2,1)} async-done(((bf16[256,1024]{1,0:T(8,128)(2,1)}), bf16[1024,1024]{1,0:T(8,128)(2,1)}) %all-gather.13.cloned.1.call-update) | async-done | bytes 2097168 | tf_op jit(solution)/shard_map/all_gather | solution.py:575
  342.7 5.2 fusion.28
  348.0 20.7 %all-gather.17.cloned.1.call-done = bf16[1024,704]{0,1:T(8,128)(2,1)} async-done(((bf16[128,704]{0,1:T(8,128)(2,1)}), bf16[1024,704]{0,1:T(8,128)(2,1)}) %all-gather.17.cloned.1.call-update) | async-done | bytes 1441808 | tf_op jit(solution)/shard_map/all_gather | solution.py:539
  368.7 5.3 fusion.29
  373.9 22.1 %all-gather.19.cloned.1.call-done = bf16[704,1024]{1,0:T(8,128)(2,1)} async-done(((bf16[704,128]{1,0:T(8,128)(2,1)}), bf16[704,1024]{1,0:T(8,128)(2,1)}) %all-gather.19.cloned.1.call-update) | async-done | bytes 1441808 | tf_op jit(solution)/shard_map/all_gather | solution.py:540
  396.0 47.6 %all-gather.21.cloned.1.call-done = bf16[1024,1024]{1,0:T(8,128)(2,1)} async-done(((bf16[256,1024]{1,0:T(8,128)(2,1)}), bf16[1024,1024]{1,0:T(8,128)(2,1)}) %all-gather.21.cloned.1.call-update) | async-done | bytes 2097168 | tf_op jit(solution)/shard_map/all_gather | solution.py:588
  443.7 7.7 multiply_convert_fusion
  453.7 3.9 convolution_add_fusion
  457.7 75.6 %reduce-scatter.22.cloned.1.call-done = f32[256,1024]{1,0:T(8,128)} async-done(((f32[1024,1024]{1,0:T(8,128)}), f32[256,1024]{1,0:T(8,128)}) %reduce-scatter.22.cloned.1.call-update) | async-done | bytes 1048592 | tf_op jit(solution)/shard_map/reduce_scatter | solution.py:591
  538.2 4.8 convolution_convert_fusion.3
  545.9 5.0 convolution_convert_fusion.4
  553.5 4.8 convolution_convert_fusion.5
  561.0 23.8 %all-gather.23.cloned.1.call-done = bf16[1024,1024]{1,0:T(8,128)(2,1)} async-done(((bf16[256,1024]{1,0:T(8,128)(2,1)}), bf16[1024,1024]{1,0:T(8,128)(2,1)}) %all-gather.23.cloned.1.call-update) | async-done | bytes 2097168 | tf_op jit(solution)/shard_map/all_gather | solution.py:619
  584.7 3.1 convolution_convert_fusion.6
  592.5 51.4 %mixer_backward.1 = (bf16[1024,1664]{1,0:T(8,128)(2,1)}, f32[4,1280]{1,0:T(4,128)S(1)}, f32[1,128]{1,0:T(1,128)S(1)}, f32[1,128]{1,0:T(1,128)}) custom-call(f32[1024,256]{1,0:T(8,128)S(1)} %fusion.31.grad_ref, f32[1024,1664]{1,0:T(8,128)} %fusion.26.raw_ref, f32[1024,16]{1,0:T(8,128)S(1)} %copy.54.aux_ref, f32[16,1,128]{2,1,0:T(1,128)S(1)} %bitcast.53, ...), custom_call_target="tpu_custom_call" | custom-call | tf_op jit(solution)/shard_map/mixer_backward/pallas_call | solution.py:426
  643.9 7.3 convolution_convert_fusion.1
  652.6 3.2 convolution_convert_fusion.2
  657.4 7.4 convolution_convert_fusion
  669.0 39.8 %reduce-scatter.34.cloned.1.call-done = bf16[128,704]{1,0:T(8,128)(2,1)} async-done(((bf16[1024,704]{1,0:T(8,128)(2,1)}), bf16[128,704]{1,0:T(8,128)(2,1)}) %reduce-scatter.34.cloned.1.call-update) | async-done | bytes 180240
  711.3 34.5 %reduce-scatter.28.cloned.1.call-done = bf16[128,256]{1,0:T(8,128)(2,1)} async-done(((bf16[1024,256]{1,0:T(8,128)(2,1)}), bf16[128,256]{1,0:T(8,128)(2,1)}) %reduce-scatter.28.cloned.1.call-update) | async-done | bytes 65552
  747.4 44.5 %reduce-scatter.24.cloned.1.call-done = bf16[256,1024]{1,0:T(8,128)(2,1)} async-done(((bf16[1024,1024]{1,0:T(8,128)(2,1)}), bf16[256,1024]{1,0:T(8,128)(2,1)}) %reduce-scatter.24.cloned.1.call-update) | async-done | bytes 524304 | tf_op jit(solution)/shard_map/reduce_scatter | solution.py:627
  794.1 43.2 %reduce-scatter.20.cloned.1.call-done = bf16[256,1024]{1,0:T(8,128)(2,1)} async-done(((bf16[1024,1024]{1,0:T(8,128)(2,1)}), bf16[256,1024]{1,0:T(8,128)(2,1)}) %reduce-scatter.20.cloned.1.call-update) | async-done | bytes 524304 | tf_op jit(solution)/shard_map/reduce_scatter | solution.py:581
  837.3 2.9 fusion.6
  840.3 47.6 %reduce-scatter.26.cloned.1.call-done = bf16[128,1664]{1,0:T(8,128)(2,1)} async-done(((bf16[1024,1664]{1,0:T(8,128)(2,1)}), bf16[128,1664]{1,0:T(8,128)(2,1)}) %reduce-scatter.26.cloned.1.call-update) | async-done | bytes 426000 | tf_op jit(solution)/shard_map/reduce_scatter | solution.py:633
  892.7 126.1 %all-reduce.12.cloned.1.call-done = (f32[1024]{0:T(1024)}, f32[4,1024]{1,0:T(4,128)}, f32[4,2048]{1,0:T(4,128)}, f32[4,2048]{1,0:T(4,128)}, f32[8]{0:T(128)}, /*index=5*/f32[128]{0:T(128)}, f32[1024]{0:T(1024)}) async-done(((f32[1024]{0:T(1024)}, f32[4,1024]{1,0:T(4,128)}, f32[4,2048]{1,0:T(4,128)}, f32[4,2048]{1,0:T(4,128)}, f32[8]{0:T(128)}, /*index=5*/f32[128]{0:T(128)}, f32[1024]{0:T(1024)}), ...) | async-done | bytes 90672 | tf_op jit(solution)/shard_map/psum | solution.py:664
  (189 shorter events, 63.9 us)
Async XLA Ops:
  7.3 52.3 %all-gather.9.cloned.1.call-start = ((), (), s32[]{:S(2)}) async-start(), calls=%async_computation.9 | async-start | bytes 2621440 | tf_op jit(solution)/shard_map/all_gather | solution.py:549
  10.7 83.4 %all-gather.11.cloned.1.call-start = ((), (), s32[]{:S(2)}) async-start(), calls=%async_computation.10 | async-start | bytes 3833856 | tf_op jit(solution)/shard_map/all_gather | solution.py:536
  11.8 255.1 %reduce-scatter.18.cloned.1.call-start = ((), (), s32[]{:S(2)}) async-start(), calls=%async_computation.11 | async-start | bytes 5242880 | tf_op jit(solution)/shard_map/reduce_scatter | solution.py:566
  26.8 76.8 %copy-start.4 = (f32[128]{0:T(128)S(1)}, f32[128]{0:T(128)}, u32[]{:S(2)}) copy-start(f32[128]{0:T(128)} %param.32) | copy-start | bytes 1540
  103.6 83.8 %copy-start.12 = (bf16[256,1024]{1,0:T(8,128)(2,1)S(1)}, bf16[256,1024]{1,0:T(8,128)(2,1)}, u32[]{:S(2)}) copy-start(bf16[256,1024]{1,0:T(8,128)(2,1)} %all_gather.29) | copy-start | bytes 1572868
  190.1 79.5 %copy-start.18 = (f32[1024]{0:T(1024)S(1)}, f32[1024]{0:T(1024)}, u32[]{:S(2)}) copy-start(f32[1024]{0:T(1024)} %param.34) | copy-start | bytes 12292
  190.1 104.6 %all-gather.15.cloned.1.call-start = ((), (), s32[]{:S(2)}) async-start(), calls=%async_computation.13 | async-start | bytes 1622016 | tf_op jit(solution)/shard_map/all_gather | solution.py:538
  190.6 152.1 %all-gather.13.cloned.1.call-start = ((), (), s32[]{:S(2)}) async-start(), calls=%async_computation.12 | async-start | bytes 2621440 | tf_op jit(solution)/shard_map/all_gather | solution.py:575
  270.5 98.2 %all-gather.17.cloned.1.call-start = ((), (), s32[]{:S(2)}) async-start(), calls=%async_computation.14 | async-start | bytes 1622016 | tf_op jit(solution)/shard_map/all_gather | solution.py:539
  271.1 125.0 %all-gather.19.cloned.1.call-start = ((), (), s32[]{:S(2)}) async-start(), calls=%async_computation.15 | async-start | bytes 1622016 | tf_op jit(solution)/shard_map/all_gather | solution.py:540
  271.8 171.8 %all-gather.21.cloned.1.call-start = ((), (), s32[]{:S(2)}) async-start(), calls=%async_computation.17 | async-start | bytes 2621440 | tf_op jit(solution)/shard_map/all_gather | solution.py:588
  272.6 260.7 %reduce-scatter.22.cloned.1.call-start = ((), (), s32[]{:S(2)}) async-start(), calls=%async_computation.18 | async-start | bytes 5242880 | tf_op jit(solution)/shard_map/reduce_scatter | solution.py:591
  457.6 127.1 %all-gather.23.cloned.1.call-start = ((), (), s32[]{:S(2)}) async-start(), calls=%async_computation.19 | async-start | bytes 2621440 | tf_op jit(solution)/shard_map/all_gather | solution.py:619
  538.1 126.8 %reduce-scatter.32.cloned.1.call-start = ((), (), s32[]{:S(2)}) async-start(), calls=%async_computation.24 | async-start | bytes 1769472
  545.6 121.4 %reduce-scatter.30.cloned.1.call-start = ((), (), s32[]{:S(2)}) async-start(), calls=%async_computation.23 | async-start | bytes 1769472
  553.5 155.3 %reduce-scatter.34.cloned.1.call-start = ((), (), s32[]{:S(2)}) async-start(), calls=%async_computation.25 | async-start | bytes 1769472
  560.9 184.9 %reduce-scatter.28.cloned.1.call-start = ((), (), s32[]{:S(2)}) async-start(), calls=%async_computation.22 | async-start | bytes 589824
  589.9 202.1 %reduce-scatter.24.cloned.1.call-start = ((), (), s32[]{:S(2)}) async-start(), calls=%async_computation.20 | async-start | bytes 2621440 | tf_op jit(solution)/shard_map/reduce_scatter | solution.py:627
  592.5 51.4 %copy-start.27 = (bf16[1024,1664]{1,0:T(8,128)(2,1)S(1)}, bf16[1024,1664]{1,0:T(8,128)(2,1)}, u32[]{:S(2)}) copy-start(bf16[1024,1664]{1,0:T(8,128)(2,1)} %all-gather.11.cloned.1.call-done) | copy-start | bytes 10223620
  651.3 186.1 %reduce-scatter.20.cloned.1.call-start = ((), (), s32[]{:S(2)}) async-start(), calls=%async_computation.16 | async-start | bytes 2621440 | tf_op jit(solution)/shard_map/reduce_scatter | solution.py:581
  655.8 232.0 %reduce-scatter.26.cloned.1.call-start = ((), (), s32[]{:S(2)}) async-start(), calls=%async_computation.21 | async-start | bytes 3833856 | tf_op jit(solution)/shard_map/reduce_scatter | solution.py:633
  664.9 127.1 %copy-start.8 = (bf16[256,1024]{1,0:T(8,128)(2,1)S(1)}, bf16[256,1024]{1,0:T(8,128)(2,1)}, u32[]{:S(2)}) copy-start(bf16[256,1024]{1,0:T(8,128)(2,1)} %param.19) | copy-start | bytes 1572868
  664.9 127.1 %copy-start.23 = (f32[1024]{0:T(1024)S(1)}, f32[1024]{0:T(1024)}, u32[]{:S(2)}) copy-start(f32[1024]{0:T(1024)} %param.22) | copy-start | bytes 12292
  664.9 353.9 %all-reduce.12.cloned.1.call-start = ((), (), s32[]{:S(2)}) async-start(), calls=%async_computation.26 | async-start | bytes 182272 | tf_op jit(solution)/shard_map/psum | solution.py:664
  666.1 171.2 %copy-start.7 = (f32[256,1024]{1,0:T(8,128)S(1)}, f32[256,1024]{1,0:T(8,128)}, u32[]{:S(2)}) copy-start(f32[256,1024]{1,0:T(8,128)} %copy-done.5) | copy-start | bytes 3145732
  666.2 171.2 %copy-start.10 = (f32[256,1024]{1,0:T(8,128)S(1)}, f32[256,1024]{1,0:T(8,128)}, u32[]{:S(2)}) copy-start(f32[256,1024]{1,0:T(8,128)} %reduce-scatter.22.cloned.1.call-done) | copy-start | bytes 3145732
  666.2 171.2 %copy-start.11 = (bf16[256,1024]{1,0:T(8,128)(2,1)S(1)}, bf16[256,1024]{1,0:T(8,128)(2,1)}, u32[]{:S(2)}) copy-start(bf16[256,1024]{1,0:T(8,128)(2,1)} %param.20) | copy-start | bytes 1572868
  711.1 82.9 %copy-start.26 = (f32[8]{0:T(128)}, f32[8]{0:T(128)S(1)}, u32[]{:S(2)}) copy-start(f32[8]{0:T(128)S(1)} %dynamic_update_slice.15) | copy-start | bytes 100
  711.2 82.9 %copy-start.22 = (f32[4,1024]{1,0:T(4,128)}, f32[4,1024]{1,0:T(4,128)S(1)}, u32[]{:S(2)}) copy-start(f32[4,1024]{1,0:T(4,128)S(1)} %slice_dynamic-update-slice_fusion.2) | copy-start | bytes 49156
  711.2 82.9 %copy-start.17 = (f32[4,2048]{1,0:T(4,128)}, f32[4,2048]{1,0:T(4,128)S(1)}, u32[]{:S(2)}) copy-start(f32[4,2048]{1,0:T(4,128)S(1)} %slice_dynamic-update-slice_fusion) | copy-start | bytes 98308
  711.3 82.8 %copy-start.16 = (f32[4,2048]{1,0:T(4,128)}, f32[4,2048]{1,0:T(4,128)S(1)}, u32[]{:S(2)}) copy-start(f32[4,2048]{1,0:T(4,128)S(1)} %slice_dynamic-update-slice_fusion.1) | copy-start | bytes 98308
  837.3 190.4 %copy-start.1 = (f32[4,1024]{1,0:T(4,128)S(1)}, f32[4,1024]{1,0:T(4,128)}, u32[]{:S(2)}) copy-start(f32[4,1024]{1,0:T(4,128)} %param.28) | copy-start | bytes 49156
  (22 other events, 77.4 us)
Sparse Core Ops, SparseCore 0:
  10.9 48.6 all-gather.8
  62.0 32.1 all-gather.10
  190.2 76.7 reduce-scatter.17
  268.9 25.7 all-gather.14
  296.8 45.9 all-gather.12
  344.6 24.0 all-gather.16
  370.7 25.2 all-gather.18
  397.7 45.9 all-gather.20
  457.8 75.4 reduce-scatter.21
  538.3 46.4 all-gather.22
  588.0 37.2 reduce-scatter.31
  628.4 38.5 reduce-scatter.29
  670.3 38.4 reduce-scatter.33
  711.7 34.1 reduce-scatter.27
  748.1 43.8 reduce-scatter.23
  794.1 43.1 reduce-scatter.19
  841.0 46.7 reduce-scatter.25
  895.3 123.4 all-reduce.11

commit v2 on v1

v2 whole, which is shorter than its diff:
```python
from functools import partial

import jax
import jax.numpy as jnp
from jax import lax
from jax.experimental import pallas as pl
from jax.experimental.pallas import tpu as pltpu
from jax.sharding import PartitionSpec as P

HEAD_DIM = 128
EPS = 1e-06
EXACT = lax.Precision.HIGHEST
HIGH = lax.Precision.HIGH
FAST = lax.Precision.DEFAULT
NN = ((1,), (0,))
NT = ((1,), (1,))
TN = ((0,), (0,))
LANE = 128
CHUNK = 64
ROWS = 2 * CHUNK
FWD_CHUNKS = 4
BWD_CHUNKS = 2


def mm(left, right, dims=NN, precision=HIGH):
    return lax.dot_general(
        left, right, (dims, ((), ())), precision=precision, preferred_element_type=jnp.float32
    )


def softplus(x):
    return jnp.maximum(x, 0.0) + jnp.log1p(jnp.exp(-jnp.abs(x)))


def chunk_masks():
    row = lax.broadcasted_iota(jnp.int32, (ROWS, ROWS), 0)
    col = lax.broadcasted_iota(jnp.int32, (ROWS, ROWS), 1)
    row_tok, col_tok = row & (CHUNK - 1), col & (CHUNK - 1)
    later = row_tok > col_tok
    same_tok = row_tok == col_tok
    pair = same_tok & (row > col)
    levels = []
    size = 1
    while size < CHUNK:
        upper = (row_tok & size) > (col_tok & size)
        together = (row_tok & (-2 * size)) == (col_tok & (-2 * size))
        levels.append(upper & together)
        size *= 2
    return row, col, later | same_tok, later | pair, pair, levels


def invert(lowers, ident, pair, levels, precision):
    inverses = [ident - jnp.where(pair, lower, 0.0) for lower in lowers]
    for level in levels:
        steps = [
            mm(jnp.where(level, lower, 0.0), inverse, NN, precision)
            for lower, inverse in zip(lowers, inverses)
        ]
        inverses = [
            inverse - mm(inverse, step, NN, precision) for inverse, step in zip(inverses, steps)
        ]
    return inverses


def col_sum(x):
    return jnp.sum(x, axis=-1, keepdims=True)


def twice(x):
    return jnp.concatenate([x, x], axis=0)


def unit_slices(heads, head):
    names = [heads + 2 * head, heads + 2 * head + 1, 3 * heads + 2 * head, 3 * heads + 2 * head + 1]
    names += [head, 5 * heads + head]
    return [slice(n * HEAD_DIM, (n + 1) * HEAD_DIM) for n in names]


def decays_of(cumul, cumul_t, beta_rows, aux, same, lane):
    c_tok = cumul[:, lane + 2 : lane + 3]
    c_end = cumul[CHUNK - 1 :, lane + 2 : lane + 3]
    decay = jnp.where(
        same, jnp.exp(jnp.minimum(twice(c_tok) - cumul_t[lane + 2 : lane + 3, :], 0.0)), 0.0
    )
    beta = jnp.concatenate(
        [beta_rows[:, lane : lane + 1], beta_rows[:, lane + 1 : lane + 2]], axis=0
    )
    start = aux[:, 0:1] * jnp.exp(c_tok)
    final = twice(aux[:, 1:2] * jnp.exp(c_end - c_tok))
    total = aux[CHUNK - 1 :, 0:1] * jnp.exp(c_end)
    return decay, beta, start, final, total


def fwd_kernel(
    heads, per_step, raw_ref, aux_ref, segrow_ref, taps_ref, bias_ref, gain_ref,
    mixed_ref, pre_ref, recall_ref, inv_ref, prox_ref, state_ref, move_ref, probe_ref,
    mem_ref, tail_ref, act_ref,
):
    width = HEAD_DIM
    block = per_step * CHUNK

    @pl.when(pl.program_id(0) == 0)
    def _():
        mem_ref[...] = jnp.zeros_like(mem_ref)
        tail_ref[...] = jnp.zeros_like(tail_ref)

    masks = [aux_ref[:, 2 + s : 3 + s] for s in range(3)]
    for tile in range(5 * heads):
        cols = slice(tile * width, (tile + 1) * width)
        raw = raw_ref[:, cols]
        joined = jnp.concatenate([tail_ref[:, cols], raw], axis=0)
        pre = raw * taps_ref[0:1, cols]
        for s in range(1, 4):
            shifted = pltpu.roll(joined, s, 0)[8:]
            pre = pre + shifted * masks[s - 1] * taps_ref[s : s + 1, cols]
        pre_ref[:, cols] = pre
        tail_ref[:, cols] = raw[block - 8 :]
        act = pre * jax.nn.sigmoid(pre)
        if tile < 3 * heads:
            act = act * lax.rsqrt(col_sum(act * act) + EPS)
        act_ref[:, cols] = act

    row, col, lower_eq, strict, pair, levels = chunk_masks()
    ident = (row == col).astype(jnp.float32)
    tri = (row[:CHUNK, :CHUNK] >= col[:CHUNK, :CHUNK]).astype(jnp.float32)
    rates = raw_ref[:, 6 * heads * width :]
    beta_tile = jax.nn.sigmoid(rates)
    log_tile = -softplus(rates + bias_ref[...])
    units = [(part, head) for part in range(per_step) for head in range(heads)]
    spans = [slice(part * CHUNK, (part + 1) * CHUNK) for part in range(per_step)]
    cumuls = [mm(tri, log_tile[rows], NN, EXACT) for rows in spans]
    cumul_ts = [twice(cumul).T for cumul in cumuls]
    sames = [
        (twice(aux_ref[rows, 8:9]) == segrow_ref[part]) & lower_eq
        for part, rows in enumerate(spans)
    ]
    keys, queries, decays, lowers, scores = [], [], [], [], []
    for part, head in units:
        k1, k2, v1, v2, q0, g0 = unit_slices(heads, head)
        rows = spans[part]
        key = jnp.concatenate([act_ref[rows, k1], act_ref[rows, k2]], axis=0)
        query = act_ref[rows, q0]
        decay = decays_of(
            cumuls[part], cumul_ts[part], beta_tile[rows], aux_ref[rows], sames[part], 3 * head
        )
        dots = mm(jnp.concatenate([key, query], axis=0), key, NT)
        keys.append(key)
        queries.append(query)
        decays.append(decay)
        lowers.append(jnp.where(strict, decay[1] * decay[0] * dots[:ROWS], 0.0))
        scores.append(decay[0][CHUNK:] * dots[ROWS:])
    inverses = invert(lowers, ident, pair, levels, HIGH)
    solved = []
    for u, (part, head) in enumerate(units):
        k1, k2, v1, v2, q0, g0 = unit_slices(heads, head)
        rows = spans[part]
        decay, beta, start, final, total = decays[u]
        inv_ref[u] = inverses[u]
        value = jnp.concatenate([act_ref[rows, v1], act_ref[rows, v2]], axis=0)
        solved.append(
            mm(
                inverses[u],
                jnp.concatenate([beta * value, beta * twice(start) * keys[u]], axis=1),
            )
        )
    moves = [mm(decays[u][3] * keys[u], solved[u], TN) for u in range(len(units))]
    reads = [mm(scores[u], solved[u]) for u in range(len(units))]
    for u, (part, head) in enumerate(units):
        memory = mem_ref[head]
        state_ref[u] = memory
        move_ref[u] = moves[u][:, width:]
        mem_ref[head] = (
            decays[u][4] * memory + moves[u][:, :width] - mm(moves[u][:, width:], memory)
        )
    for u, (part, head) in enumerate(units):
        probe = decays[u][2] * queries[u] - reads[u][:, width:]
        probe_ref[u] = probe
        seen = mm(jnp.concatenate([solved[u][:, width:], probe], axis=0), state_ref[u])
        prox_ref[u] = solved[u][:, :width] - seen[:ROWS]
        recall = reads[u][:, :width] + seen[ROWS:]
        rows = spans[part]
        cols = slice(head * width, (head + 1) * width)
        recall_ref[rows, cols] = recall
        scale = lax.rsqrt(jnp.mean(recall * recall, axis=-1, keepdims=True) + EPS)
        gate = raw_ref[rows, unit_slices(heads, head)[5]]
        mixed = recall * scale * gain_ref[...] * (gate * jax.nn.sigmoid(gate))
        mixed_ref[rows, cols] = mixed.astype(jnp.bfloat16)


def bwd_kernel(
    heads, per_step, grad_ref, raw_ref, aux_ref, segrow_ref, pre_ref, recall_ref, inv_ref,
    prox_ref, state_ref, move_ref, probe_ref, taps_ref, bias_ref, gain_ref,
    low_ref, taps_grad_ref, bias_grad_ref, gain_grad_ref,
    adj_ref, head_ref, act_ref, norm_ref, dact_ref, keep_ref,
):
    width = HEAD_DIM
    block = per_step * CHUNK

    @pl.when(pl.program_id(0) == 0)
    def _():
        adj_ref[...] = jnp.zeros_like(adj_ref)
        head_ref[...] = jnp.zeros_like(head_ref)
        taps_grad_ref[...] = jnp.zeros_like(taps_grad_ref)
        bias_grad_ref[...] = jnp.zeros_like(bias_grad_ref)
        gain_grad_ref[...] = jnp.zeros_like(gain_grad_ref)

    row, col, lower_eq, strict, pair, levels = chunk_masks()
    tri = (row[:CHUNK, :CHUNK] >= col[:CHUNK, :CHUNK]).astype(jnp.float32)
    tri_t = (row[:CHUNK, :CHUNK] <= col[:CHUNK, :CHUNK]).astype(jnp.float32)
    lanes = col[:CHUNK, :]
    rates = raw_ref[:, 6 * heads * width :]
    beta_tile = jax.nn.sigmoid(rates)
    keep_in = rates + bias_ref[...]
    log_tile = -softplus(keep_in)
    units = [(part, head) for part in reversed(range(per_step)) for head in range(heads)]
    spans = [slice(part * CHUNK, (part + 1) * CHUNK) for part in range(per_step)]
    cumuls = [mm(tri, log_tile[rows], NN, EXACT) for rows in spans]
    cumul_ts = [twice(cumul).T for cumul in cumuls]
    sames = [
        (twice(aux_ref[rows, 8:9]) == segrow_ref[part]) & lower_eq
        for part, rows in enumerate(spans)
    ]
    gain_total = jnp.zeros((1, width), jnp.float32)
    out_grads = []
    for part, head in units:
        rows = spans[part]
        q0, g0 = unit_slices(heads, head)[4:]
        recall = recall_ref[rows, q0]
        grad = grad_ref[rows, q0].astype(jnp.float32)
        gate = raw_ref[rows, g0]
        gate_sig = jax.nn.sigmoid(gate)
        silu_gate = gate * gate_sig
        scale = lax.rsqrt(jnp.mean(recall * recall, axis=-1, keepdims=True) + EPS)
        normed = recall * scale
        gain_total = gain_total + jnp.sum(grad * normed * silu_gate, axis=0, keepdims=True)
        weighted = grad * gain_ref[...]
        low_ref[rows, g0] = (
            weighted * normed * gate_sig * (1.0 + gate * (1.0 - gate_sig))
        ).astype(jnp.bfloat16)
        normed_grad = weighted * silu_gate
        out_grads.append(
            scale * (normed_grad - normed * jnp.mean(normed_grad * normed, axis=-1, keepdims=True))
        )
    gain_grad_ref[...] += gain_total
    reads = [
        mm(probe_ref[part * heads + head], out_grads[u], TN) for u, (part, head) in enumerate(units)
    ]
    for u, (part, head) in enumerate(units):
        spot = part * heads + head
        c_end = cumuls[part][CHUNK - 1 :, 3 * head + 2 : 3 * head + 3]
        total = aux_ref[(part + 1) * CHUNK - 1 : (part + 1) * CHUNK, 0:1] * jnp.exp(c_end)
        adjoint = adj_ref[head]
        keep_ref[spot] = adjoint
        adj_ref[head] = total * adjoint + reads[u] - mm(move_ref[spot], adjoint, TN)
    for tile in range(5 * heads):
        cols = slice(tile * width, (tile + 1) * width)
        pre = pre_ref[:, cols]
        act = pre * jax.nn.sigmoid(pre)
        if tile < 3 * heads:
            scale = lax.rsqrt(col_sum(act * act) + EPS)
            norm_ref[:, cols] = jnp.broadcast_to(scale, act.shape)
            act = act * scale
        act_ref[:, cols] = act
    keys, decays, dots = [], [], []
    for u, (part, head) in enumerate(units):
        k1, k2, v1, v2, q0, g0 = unit_slices(heads, head)
        rows = spans[part]
        key = jnp.concatenate([act_ref[rows, k1], act_ref[rows, k2]], axis=0)
        keys.append(key)
        decays.append(
            decays_of(
                cumuls[part], cumul_ts[part], beta_tile[rows], aux_ref[rows], sames[part], 3 * head
            )
        )
        dots.append(mm(jnp.concatenate([key, act_ref[rows, q0]], axis=0), key, NT))
    scores = [decays[u][0][CHUNK:] * dots[u][ROWS:] for u in range(len(units))]
    proxy_grads = [
        mm(scores[u], out_grads[u], TN)
        + mm(decays[u][3] * keys[u], keep_ref[part * heads + head])
        for u, (part, head) in enumerate(units)
    ]
    both_grads = [
        jnp.concatenate(
            [mm(inv_ref[part * heads + head], proxy_grads[u], TN), out_grads[u]], axis=0
        )
        for u, (part, head) in enumerate(units)
    ]
    outers = [
        mm(both_grads[u], prox_ref[part * heads + head], NT)
        for u, (part, head) in enumerate(units)
    ]
    throughs = [
        mm(both_grads[u], state_ref[part * heads + head], NT)
        for u, (part, head) in enumerate(units)
    ]
    finals = [
        decays[u][3] * mm(prox_ref[part * heads + head], keep_ref[part * heads + head], NT)
        for u, (part, head) in enumerate(units)
    ]
    score_grads, inners, beta_parts, log_cols = [], [], [], []
    for u, (part, head) in enumerate(units):
        decay, beta, start, final, total = decays[u]
        key_decay = jnp.where(strict, decay * dots[u][:ROWS], 0.0)
        lower_grad = -outers[u][:ROWS]
        beta_part = lower_grad * key_decay
        dots_grad = jnp.where(strict, lower_grad * beta * decay, 0.0)
        score_grad = outers[u][ROWS:] * decay[CHUNK:]
        log_part = beta_part * beta
        log_part = jnp.concatenate(
            [log_part[:CHUNK], log_part[CHUNK:] + outers[u][ROWS:] * scores[u]], axis=0
        )
        log_cols.append(col_sum(log_part - log_part.T))
        beta_parts.append(col_sum(beta_part))
        score_grads.append(score_grad)
        inners.append(
            mm(jnp.concatenate([dots_grad + dots_grad.T, score_grad], axis=0), keys[u])
        )
    zero = jnp.zeros((CHUNK, width), jnp.float32)
    beta_grads, cumul_grads, end_grads = [zero] * per_step, [zero] * per_step, [zero] * per_step
    for u, (part, head) in enumerate(units):
        k1, k2, v1, v2, q0, g0 = unit_slices(heads, head)
        rows = spans[part]
        spot = part * heads + head
        lane = 3 * head
        decay, beta, start, final, total = decays[u]
        through, final_part, right_grad = throughs[u], finals[u], both_grads[u][:ROWS]
        query = act_ref[rows, q0]
        value = jnp.concatenate([act_ref[rows, v1], act_ref[rows, v2]], axis=0)
        beta_start = beta * twice(start)
        key_through = col_sum(keys[u] * through[:ROWS])
        query_through = start * col_sum(query * through[ROWS:])
        final_sum = col_sum(keys[u] * final_part)
        key_grad = (
            inners[u][:ROWS]
            + mm(score_grads[u], query, TN)
            - beta_start * through[:ROWS]
            + final_part
        )
        dact_ref[rows, k1] = key_grad[:CHUNK]
        dact_ref[rows, k2] = key_grad[CHUNK:]
        value_grad = beta * right_grad
        dact_ref[rows, v1] = value_grad[:CHUNK]
        dact_ref[rows, v2] = value_grad[CHUNK:]
        dact_ref[rows, q0] = inners[u][ROWS:] + start * through[ROWS:]
        beta_col = col_sum(right_grad * value) - twice(start) * key_through + beta_parts[u]
        c_grad = log_cols[u] - beta_start * key_through - final_sum
        c_grad = c_grad[:CHUNK] + c_grad[CHUNK:] + query_through
        end_part = jnp.sum(final_sum, axis=0, keepdims=True) + total * jnp.sum(
            col_sum(state_ref[spot] * keep_ref[spot]), axis=0, keepdims=True
        )
        beta_grads[part] = jnp.where(
            lanes == lane,
            beta_col[:CHUNK],
            jnp.where(lanes == lane + 1, beta_col[CHUNK:], beta_grads[part]),
        )
        cumul_grads[part] = jnp.where(lanes == lane + 2, c_grad, cumul_grads[part])
        end_grads[part] = jnp.where(lanes == lane + 2, end_part, end_grads[part])
    bias_total = jnp.zeros((1, width), jnp.float32)
    for part, rows in enumerate(spans):
        log_grad = mm(tri_t, cumul_grads[part], NN, EXACT) + end_grads[part]
        beta_rows = beta_tile[rows]
        keep_grad = -log_grad * jax.nn.sigmoid(keep_in[rows]) * aux_ref[rows, 2:3]
        rate_grad = beta_grads[part] * beta_rows * (1.0 - beta_rows) + keep_grad
        bias_total = bias_total + jnp.sum(keep_grad, axis=0, keepdims=True)
        low_ref[rows, 6 * heads * width :] = rate_grad.astype(jnp.bfloat16)
    bias_grad_ref[...] += bias_total

    masks = [aux_ref[:, 5 + s : 6 + s] for s in range(3)]
    for tile in range(5 * heads):
        cols = slice(tile * width, (tile + 1) * width)
        pre = pre_ref[:, cols]
        sig = jax.nn.sigmoid(pre)
        grad = dact_ref[:, cols]
        if tile < 3 * heads:
            act = act_ref[:, cols]
            grad = norm_ref[:, cols] * (grad - act * col_sum(grad * act))
        grad = grad * sig * (1.0 + pre * (1.0 - sig))
        raw = raw_ref[:, cols]
        joined = jnp.concatenate([grad, head_ref[:, cols]], axis=0)
        head_ref[:, cols] = grad[:8]
        raw_grad = grad * taps_ref[0:1, cols]
        taps_grad_ref[0:1, cols] += jnp.sum(raw * grad, axis=0, keepdims=True)
        for s in range(1, 4):
            shifted = pltpu.roll(joined, block + 8 - s, 0)[:block] * masks[s - 1]
            raw_grad = raw_grad + shifted * taps_ref[s : s + 1, cols]
            taps_grad_ref[s : s + 1, cols] += jnp.sum(raw * shifted, axis=0, keepdims=True)
        low_ref[:, cols] = raw_grad.astype(jnp.bfloat16)


def token_aux(segments):
    length = segments.shape[0]
    seg = segments.astype(jnp.int32)
    chunks = seg.reshape(length // CHUNK, CHUNK)
    last = chunks[:, -1]
    before = jnp.concatenate([jnp.full((1,), -1, jnp.int32), last[:-1]])
    columns = [
        (chunks == before[:, None]).reshape(length),
        (chunks == last[:, None]).reshape(length),
    ]
    for s in range(1, 4):
        columns.append(jnp.pad(seg, (s, 0), constant_values=-1)[:length] == seg)
    for s in range(1, 4):
        columns.append(jnp.pad(seg, (0, s), constant_values=-1)[s:] == seg)
    columns.append(seg)
    columns += [jnp.zeros_like(seg)] * 7
    aux = jnp.stack([c.astype(jnp.float32) for c in columns], axis=1)
    row = chunks.astype(jnp.float32)
    return aux, jnp.concatenate([row, row], axis=1)[:, None, :]


def mixer_forward(raw, aux, segrow, taps, bias, gain, heads, per_step):
    length = raw.shape[0]
    width = HEAD_DIM
    block = per_step * CHUNK
    steps = length // block
    units = per_step * heads
    total_units = steps * units
    cols = raw.shape[1]
    f32 = jnp.float32
    tiles = lambda i: (i, 0)
    cubes = lambda i: (i, 0, 0)
    fixed = lambda i: (0, 0)
    unit_spec = pl.BlockSpec((units, ROWS, width), cubes)
    unit_shape = jax.ShapeDtypeStruct((total_units, ROWS, width), f32)
    return pl.pallas_call(
        partial(fwd_kernel, heads, per_step),
        grid=(steps,),
        in_specs=[
            pl.BlockSpec((block, cols), tiles),
            pl.BlockSpec((block, 16), tiles),
            pl.BlockSpec((per_step, 1, ROWS), cubes),
            pl.BlockSpec(taps.shape, fixed),
            pl.BlockSpec((1, width), fixed),
            pl.BlockSpec((1, width), fixed),
        ],
        out_specs=[
            pl.BlockSpec((block, heads * width), tiles),
            pl.BlockSpec((block, 5 * heads * width), tiles),
            pl.BlockSpec((block, heads * width), tiles),
            unit_spec,
            unit_spec,
            unit_spec,
            unit_spec,
            pl.BlockSpec((units, CHUNK, width), cubes),
        ],
        out_shape=[
            jax.ShapeDtypeStruct((length, heads * width), jnp.bfloat16),
            jax.ShapeDtypeStruct((length, 5 * heads * width), f32),
            jax.ShapeDtypeStruct((length, heads * width), f32),
            unit_shape,
            unit_shape,
            unit_shape,
            unit_shape,
            jax.ShapeDtypeStruct((total_units, CHUNK, width), f32),
        ],
        scratch_shapes=[
            pltpu.VMEM((heads, width, width), f32),
            pltpu.VMEM((8, 5 * heads * width), f32),
            pltpu.VMEM((block, 5 * heads * width), f32),
        ],
        compiler_params=pltpu.CompilerParams(
            dimension_semantics=("arbitrary",), vmem_limit_bytes=48 * 1024 * 1024
        ),
        name="mixer_forward",
    )(raw, aux, segrow, taps, bias, gain)


def mixer_backward(grad, raw, aux, segrow, saved, taps, bias, gain, heads, per_step):
    pre, recall, inverse, proxy, state, move, probe = saved
    length = raw.shape[0]
    width = HEAD_DIM
    block = per_step * CHUNK
    steps = length // block
    units = per_step * heads
    cols = raw.shape[1]
    f32 = jnp.float32
    tiles = lambda i: (steps - 1 - i, 0)
    cubes = lambda i: (steps - 1 - i, 0, 0)
    fixed = lambda i: (0, 0)
    unit_spec = pl.BlockSpec((units, ROWS, width), cubes)
    return pl.pallas_call(
        partial(bwd_kernel, heads, per_step),
        grid=(steps,),
        in_specs=[
            pl.BlockSpec((block, heads * width), tiles),
            pl.BlockSpec((block, cols), tiles),
            pl.BlockSpec((block, 16), tiles),
            pl.BlockSpec((per_step, 1, ROWS), cubes),
            pl.BlockSpec((block, 5 * heads * width), tiles),
            pl.BlockSpec((block, heads * width), tiles),
            unit_spec,
            unit_spec,
            unit_spec,
            unit_spec,
            pl.BlockSpec((units, CHUNK, width), cubes),
            pl.BlockSpec(taps.shape, fixed),
            pl.BlockSpec((1, width), fixed),
            pl.BlockSpec((1, width), fixed),
        ],
        out_specs=[
            pl.BlockSpec((block, cols), tiles),
            pl.BlockSpec(taps.shape, fixed),
            pl.BlockSpec((1, width), fixed),
            pl.BlockSpec((1, width), fixed),
        ],
        out_shape=[
            jax.ShapeDtypeStruct((length, cols), jnp.bfloat16),
            jax.ShapeDtypeStruct(taps.shape, f32),
            jax.ShapeDtypeStruct((1, width), f32),
            jax.ShapeDtypeStruct((1, width), f32),
        ],
        scratch_shapes=[
            pltpu.VMEM((heads, width, width), f32),
            pltpu.VMEM((8, 5 * heads * width), f32),
            pltpu.VMEM((block, 5 * heads * width), f32),
            pltpu.VMEM((block, 3 * heads * width), f32),
            pltpu.VMEM((block, 5 * heads * width), f32),
            pltpu.VMEM((units, width, width), f32),
        ],
        compiler_params=pltpu.CompilerParams(
            dimension_semantics=("arbitrary",), vmem_limit_bytes=48 * 1024 * 1024
        ),
        name="mixer_backward",
    )(grad, raw, aux, segrow, pre, recall, inverse, proxy, state, move, probe, taps, bias, gain)


def up_to(x, multiple):
    return -(-x // multiple) * multiple


def row_scale(values):
    return lax.rsqrt(jnp.mean(values * values, axis=-1, keepdims=True) + EPS)


def norm_back(grad, values, scale, gain):
    normed = values * scale
    gain_grad = jnp.sum(grad * normed, axis=0)
    weighted = grad * gain
    value_grad = scale * (weighted - normed * jnp.mean(weighted * normed, axis=-1, keepdims=True))
    return (value_grad, gain_grad)


def dot(left, right, dims=NN):
    return lax.dot_general(left, right, (dims, ((), ())), preferred_element_type=jnp.float32)


def swap(x, axis, bit):
    size = lax.axis_size(axis)
    return lax.ppermute(x, axis, [(i, i ^ bit) for i in range(size)])


def line_gather(x, axis):
    size = lax.axis_size(axis)
    index = lax.axis_index(axis)
    up = [(i, i + 1) for i in range(size - 1)]
    down = [(i + 1, i) for i in range(size - 1)]
    below, above = [], []
    from_below = from_above = x
    for _ in range(size - 1):
        from_below = lax.ppermute(from_below, axis, up)
        from_above = lax.ppermute(from_above, axis, down)
        below.insert(0, from_below)
        above.append(from_above)
    stacked = jnp.stack(below + [x] + above)
    return lax.dynamic_slice_in_dim(stacked, size - 1 - index, size, axis=0)


def direct_gather(x, axis):
    size = lax.axis_size(axis)
    index = lax.axis_index(axis)
    pieces = []
    for step in range(1 - size, size):
        if step == 0:
            pieces.append(x)
        else:
            pairs = [(i + step, i) for i in range(size) if 0 <= i + step < size]
            pieces.append(lax.ppermute(x, axis, pairs))
    return lax.dynamic_slice_in_dim(jnp.stack(pieces), size - 1 - index, size, axis=0)


def line_scatter(blocks, axis):
    size = lax.axis_size(axis)
    index = lax.axis_index(axis)

    def block(j):
        return lax.dynamic_index_in_dim(blocks, jnp.clip(j, 0, size - 1), 0, keepdims=False)

    up = down = None
    for step in range(1, size):
        up_next, down_next = block(index + size - step), block(index - size + step)
        if step > 1:
            up_next = (up_next.astype(jnp.float32) + up.astype(jnp.float32)).astype(blocks.dtype)
            down_next = (down_next.astype(jnp.float32) + down.astype(jnp.float32)).astype(
                blocks.dtype
            )
        up = lax.ppermute(up_next, axis, [(i, i + 1) for i in range(step)])
        down = lax.ppermute(
            down_next, axis, [(i, i - 1) for i in range(size - step, size)]
        )
    own = block(index).astype(jnp.float32)
    return own + up.astype(jnp.float32) + down.astype(jnp.float32)


def bits_of(size):
    return [1 << b for b in range(size.bit_length() - 1)]


def tree_gather(x, axis):
    size = lax.axis_size(axis)
    index = lax.axis_index(axis)
    bits = bits_of(size)
    half = x.shape[1] // 2 // LANE * LANE
    halves = []
    for part, order in ((x[:, :half], bits[:0:-1] + bits[:1]), (x[:, half:], bits[1:] + bits[:1])):
        joined = part[None]
        places = [0]
        for bit in order:
            got = swap(joined, axis, bit)
            joined = jnp.concatenate([joined, got], axis=0)
            places = places + [p ^ bit for p in places]
        halves.append((joined, places))
    out = []
    for j in range(size):
        out.append([])
        for joined, places in halves:
            where = jnp.asarray([places.index(r) for r in range(size)], jnp.int32)
            spot = lax.dynamic_index_in_dim(where, index ^ j, 0, keepdims=False)
            out[j].append(lax.dynamic_index_in_dim(joined, spot, 0, keepdims=False))
    return jnp.concatenate([jnp.concatenate(pair, axis=1) for pair in out], axis=0)


def tree_scatter(blocks, axis):
    size = lax.axis_size(axis)
    index = lax.axis_index(axis)
    bits = bits_of(size)
    cols = blocks.shape[2]
    half = cols // 2 // LANE * LANE
    out = []
    for part, order in (
        (blocks[:, :, :half], bits[:1] + bits[1:]),
        (blocks[:, :, half:], bits[:1] + bits[:0:-1]),
    ):
        rows = part.shape[1]
        held = part.reshape((2,) * len(bits) + (rows, part.shape[2]))
        left = list(reversed(bits))
        for bit in order:
            at = left.index(bit)
            mine = (index // bit) % 2
            sent = lax.dynamic_index_in_dim(held, 1 - mine, at, keepdims=False)
            kept = lax.dynamic_index_in_dim(held, mine, at, keepdims=False)
            got = swap(sent.astype(jnp.bfloat16), axis, bit)
            held = kept.astype(jnp.float32) + got.astype(jnp.float32)
            left.pop(at)
        out.append(held)
    return jnp.concatenate(out, axis=1)


def body(
    layer_input,
    cotangent,
    segments,
    mix_gain,
    query_weight,
    key_weight,
    value_weight,
    outgate_weight,
    rate_weight,
    conv_query,
    conv_key,
    conv_value,
    decay_bias,
    out_gain,
    out_weight,
    mlp_gain,
    gate_weight,
    up_weight,
    down_weight,
):
    f32, bf16 = jnp.float32, jnp.bfloat16
    head_index = lax.axis_index("head")
    n_head, n_batch = lax.axis_size("head"), lax.axis_size("batch")
    rows, width = layer_input.shape
    length = rows * n_head
    local_heads = query_weight.shape[1] // HEAD_DIM
    unit = local_heads * HEAD_DIM
    mix_cols = 6 * unit + HEAD_DIM
    ff = gate_weight.shape[1]
    ff_pad = up_to(ff, LANE)

    own_mix = jnp.concatenate(
        [
            query_weight,
            key_weight,
            value_weight,
            outgate_weight,
            jnp.pad(rate_weight, ((0, 0), (0, HEAD_DIM - rate_weight.shape[1]))),
            out_weight.T,
        ],
        axis=1,
    )
    tokens = line_gather(layer_input, "head")
    mix_w = tree_gather(own_mix, "batch")
    proj_w, own_out_t = mix_w[:, :mix_cols], mix_w[:, mix_cols:]

    pad = ((0, 0), (0, ff_pad - ff))
    own_ff = jnp.concatenate(
        [jnp.pad(gate_weight, pad), jnp.pad(up_weight, pad), jnp.pad(down_weight.T, pad)], axis=1
    )
    own_ff, tokens, mix_w_done = lax.optimization_barrier((own_ff, tokens, own_out_t))
    shards = [own_ff]
    for bit in bits_of(n_head)[1:]:
        shards = shards + [swap(shard, "head", bit) for shard in shards]
    ff_sets = [lax.all_gather(shard, "batch", axis=0, tiled=True) for shard in shards]

    all_in = tokens.reshape(length, width).astype(f32)
    scale_all = row_scale(all_in)
    rows_in = (all_in * scale_all * mix_gain).astype(bf16)
    raw = dot(rows_in, proj_w)

    def head_cols(table, per_head):
        return lax.dynamic_slice_in_dim(
            table, head_index * local_heads * per_head, local_heads * per_head, axis=table.ndim - 1
        )

    taps = jnp.concatenate(
        [
            head_cols(conv_query, HEAD_DIM),
            head_cols(conv_key, 2 * HEAD_DIM),
            head_cols(conv_value, 2 * HEAD_DIM),
        ],
        axis=1,
    )
    own_bias = head_cols(decay_bias, 1)
    bias = jnp.stack([jnp.zeros_like(own_bias), jnp.zeros_like(own_bias), own_bias], axis=1)
    bias = jnp.pad(bias.reshape(-1), (0, HEAD_DIM - 3 * local_heads))[None]
    aux, segrow = token_aux(segments)
    gain = out_gain[None]
    out_t = direct_gather(mix_w_done, "head")
    pair_grad = swap(cotangent, "head", 1)
    mixed_low, *saved = mixer_forward(raw, aux, segrow, taps, bias, gain, local_heads, FWD_CHUNKS)

    mixed_all = lax.all_to_all(
        mixed_low.reshape(n_head, rows, unit), "head", split_axis=0, concat_axis=0, tiled=True
    )
    resid_in = layer_input.astype(f32)
    resid_mid = resid_in + sum(dot(mixed_all[j], out_t[j], NT) for j in range(n_head))
    scale_mid = row_scale(resid_mid)
    normed_mid = (resid_mid * scale_mid * mlp_gain).astype(bf16)
    pair_mid = jnp.concatenate([normed_mid, swap(normed_mid, "head", 1)], axis=0)
    pair_cot = jnp.concatenate([cotangent, pair_grad], axis=0)
    out_part = mid_part = None
    ff_grads = []
    for ff_set in ff_sets:
        gate_up = dot(pair_mid, ff_set[:, : 2 * ff_pad])
        gate_pre, up_pre = gate_up[:, :ff_pad], gate_up[:, ff_pad:]
        gate_sig = jax.nn.sigmoid(gate_pre)
        silu_gate = gate_pre * gate_sig
        hidden = (silu_gate * up_pre).astype(bf16)
        hidden_grad = dot(pair_cot, ff_set[:, 2 * ff_pad :])
        gate_grad = (
            hidden_grad * up_pre * gate_sig * (1.0 + gate_pre * (1.0 - gate_sig))
        ).astype(bf16)
        up_grad = (hidden_grad * silu_gate).astype(bf16)
        both_grad = jnp.concatenate([gate_grad, up_grad], axis=1)
        out_here = dot(hidden, ff_set[:, 2 * ff_pad :], NT)
        mid_here = dot(both_grad, ff_set[:, : 2 * ff_pad], NT)
        out_part = out_here if out_part is None else out_part + out_here
        mid_part = mid_here if mid_part is None else mid_part + mid_here
        ff_grads.append((both_grad, hidden))
    mid_grad = mid_part[:rows] + swap(mid_part[rows:].astype(bf16), "head", 1).astype(f32)
    mid_back, mlp_gain_part = norm_back(mid_grad, resid_mid, scale_mid, mlp_gain)
    resid_grad = cotangent.astype(f32) + mid_back
    branch_grad = resid_grad.astype(bf16)
    mixed_grad = jnp.stack([dot(branch_grad, out_t[j]) for j in range(n_head)]).astype(bf16)
    mixed_grad = lax.all_to_all(
        mixed_grad, "head", split_axis=0, concat_axis=0, tiled=True
    ).reshape(length, unit)
    layer_output = (
        resid_mid + out_part[:rows] + swap(out_part[rows:].astype(bf16), "head", 1).astype(f32)
    ).astype(bf16)

    ff_sums = [
        lax.psum_scatter(
            jnp.concatenate([dot(pair_mid, both, TN), dot(pair_cot, hidden, TN)], axis=1).astype(
                bf16
            ),
            "batch",
            scatter_dimension=0,
            tiled=True,
        )
        for both, hidden in reversed(ff_grads)
    ]
    branch_rows, mixed_grad = lax.optimization_barrier((branch_grad, mixed_grad))
    branch_rows = direct_gather(branch_rows, "head").reshape(length, width)

    raw_low, taps_grad, bias_grad, gain_grad = mixer_backward(
        mixed_grad, raw, aux, segrow, saved, taps, bias, gain, local_heads, BWD_CHUNKS
    )
    total = dot(raw_low, proj_w, NT)
    in_grad = line_scatter(total.astype(bf16).reshape(n_head, rows, width), "head")
    mix_gain_part = jnp.sum(total * (all_in * scale_all), axis=0)
    mix_sum = jnp.concatenate([dot(rows_in, raw_low, TN), dot(branch_rows, mixed_low, TN)], axis=1)
    mix_total = tree_scatter(
        mix_sum.astype(bf16).reshape(n_batch, width // n_batch, mix_cols + unit), "batch"
    )
    in_back, _ = norm_back(in_grad, resid_in, row_scale(resid_in), mix_gain)
    input_grad = resid_grad + in_back

    ff_total = ff_sums
    for bit in reversed(bits_of(n_head)[1:]):
        half = len(ff_total) // 2
        ff_total = [
            kept.astype(f32) + swap(sent.astype(bf16), "head", bit).astype(f32)
            for sent, kept in zip(ff_total[:half], ff_total[half:])
        ]
    ff_total = ff_total[0].astype(f32)

    own_bias_grad = bias_grad[0, : 3 * local_heads].reshape(local_heads, 3)[:, 2]
    small = [
        taps_grad[:, :unit].reshape(-1),
        taps_grad[:, unit : 3 * unit].reshape(-1),
        taps_grad[:, 3 * unit :].reshape(-1),
        own_bias_grad,
        gain_grad[0],
        mlp_gain_part,
        mix_gain_part,
    ]
    lengths = [part.shape[0] for part in small]
    packed = pack(small)
    for bit in bits_of(n_batch):
        packed = packed + swap(packed, "batch", bit)
    small = unpack(packed, lengths)

    def place_cols(table_shape, local_part, per_head):
        local_part = local_part.reshape(table_shape[:-1] + (-1,))
        return lax.dynamic_update_slice_in_dim(
            jnp.zeros(table_shape, f32),
            local_part,
            head_index * local_heads * per_head,
            axis=len(table_shape) - 1,
        ).reshape(-1)

    tables = [
        place_cols(conv_query.shape, small[0], HEAD_DIM),
        place_cols(conv_key.shape, small[1], 2 * HEAD_DIM),
        place_cols(conv_value.shape, small[2], 2 * HEAD_DIM),
        place_cols(decay_bias.shape, small[3], 1),
    ] + small[4:]
    lengths = [part.shape[0] for part in tables]
    packed = pack(tables)
    for bit in bits_of(n_head):
        packed = packed + swap(packed, "head", bit)
    tables = unpack(packed, lengths)
    return (
        layer_output,
        input_grad,
        tables[6],
        mix_total[:, :unit],
        mix_total[:, unit : 3 * unit],
        mix_total[:, 3 * unit : 5 * unit],
        mix_total[:, 5 * unit : 6 * unit],
        mix_total[:, 6 * unit : 6 * unit + rate_weight.shape[1]],
        tables[0].reshape(conv_query.shape),
        tables[1].reshape(conv_key.shape),
        tables[2].reshape(conv_value.shape),
        tables[3],
        tables[4],
        mix_total[:, mix_cols:].T,
        tables[5],
        ff_total[:, :ff],
        ff_total[:, ff_pad : ff_pad + ff],
        ff_total[:, 2 * ff_pad : 2 * ff_pad + ff].T,
    )


def pack(parts):
    flat = jnp.concatenate(parts)
    return jnp.pad(flat, (0, -flat.shape[0] % (8 * LANE))).reshape(-1, LANE)


def unpack(packed, lengths):
    flat = packed.reshape(-1)
    out, at = [], 0
    for size in lengths:
        out.append(flat[at : at + size])
        at += size
    return out


def solution(mesh):
    placed = (
        P(("batch", "head"), None),
        P(("batch", "head"), None),
        P("batch"),
        P(),
        P("batch", "head"),
        P("batch", "head"),
        P("batch", "head"),
        P("batch", "head"),
        P("batch", "head"),
        P(),
        P(),
        P(),
        P(),
        P(),
        P("head", "batch"),
        P(),
        P("batch", "head"),
        P("batch", "head"),
        P("head", "batch"),
    )
    return jax.shard_map(
        body,
        mesh=mesh,
        in_specs=placed,
        out_specs=(
            P(("batch", "head"), None),
            P(("batch", "head"), None),
            P(),
            P("batch", "head"),
            P("batch", "head"),
            P("batch", "head"),
            P("batch", "head"),
            P("batch", "head"),
            P(),
            P(),
            P(),
            P(),
            P(),
            P("head", "batch"),
            P(),
            P("batch", "head"),
            P("batch", "head"),
            P("head", "batch"),
        ),
        check_vma=False,
    )
```

time: 1040 us -> 580 us (0.56)
  waiting for transfers between devices: 742 us -> 175 us
  starting transfers between devices: 1.37 us -> 92.7 us
  Pallas kernels: 134 us -> 63.3 us
  local copies, waits for them, and re-layouts: 36.8 us -> 80 us
  between operations: 15.3 us -> 46.7 us
  other arithmetic: 19 us -> 37.5 us
  blocking collectives: 12.5 us -> 0 us
    reduce_scatter x5 -> x2, waiting for transfers between devices: 287 us -> 0.01 us  [body(): lax.psum_scatter(jnp.concatenate([dot(pair_mid, both, TN), dot(pair_cot,...]
    all_gather x8 -> x2, waiting for transfers between devices: 251 us -> 0.01 us  [body(): lax.all_gather(shard, 'batch', axis=0, tiled=True)]
    ppermute x0 -> x47, waiting for transfers between devices: none -> 172 us  [the longest x23 107 us: swap(): return lax.ppermute(x, axis, [(i, i ^ bit) for i in range(size)])]
    psum x1 -> x0, waiting for transfers between devices: 126 us -> none  [body(): lax.psum((mix_gain_part, mlp_gain_part, gain_grad[0], place_cols(conv_que...]
    ppermute x0 -> x47, starting transfers between devices: none -> 85 us  [the longest x12 25.9 us: direct_gather(): pieces.append(lax.ppermute(x, axis, pairs))]
    unnamed x22 -> x4, waiting for transfers between devices: 77 us -> 0.07 us
    pallas_call x1, Pallas kernels: 82.7 us -> 29.4 us  [mixer_forward(): pl.pallas_call(partial(fwd_kernel, heads, per_step), grid=(steps,), in_sp...]
    pallas_call x1, Pallas kernels: 51.4 us -> 33.9 us  [mixer_backward(): pl.pallas_call(partial(bwd_kernel, heads, per_step), grid=(steps,), in_sp...]
  transfers between devices with their start and end apart: 18 -> 53, of which waited for: 16 -> 19; matrix products, arithmetic and copies ran while one was open for 8% -> 28% of each run, Pallas kernels for 5% -> 11%
where the time goes in v2:
time: 580 us; the launch traced here: 573 us
  waiting for transfers between devices  175 us (30%)
  starting transfers between devices  92.7 us (16%)
  local copies, waits for them, and re-layouts  80 us (14%)
  matrix products  77.6 us (13%)
  Pallas kernels  63.3 us (11%)
  between operations  46.7 us (8%)
  other arithmetic  37.5 us (6%)
    ppermute x23, waiting for transfers between devices, swap(): return lax.ppermute(x, axis, [(i, i ^ bit) for i in range(size)])  107 us
    dot_general x24, matrix products, dot(): lax.dot_general(left, right, (dims, ((), ())), preferred_element_type=jnp...  77.6 us
    unnamed x155, local copies, waits for them, and re-layouts  43.3 us
    ppermute x12, waiting for transfers between devices, direct_gather(): pieces.append(lax.ppermute(x, axis, pairs))  40.2 us
    pallas_call x1, Pallas kernels, mixer_backward(): pl.pallas_call(partial(bwd_kernel, heads, per_step), grid=(steps,), in_sp...  33.9 us
    pallas_call x1, Pallas kernels, mixer_forward(): pl.pallas_call(partial(fwd_kernel, heads, per_step), grid=(steps,), in_sp...  29.4 us
    ppermute x12, starting transfers between devices, direct_gather(): pieces.append(lax.ppermute(x, axis, pairs))  25.9 us
    ppermute x23, starting transfers between devices, swap(): return lax.ppermute(x, axis, [(i, i ^ bit) for i in range(size)])  21.3 us
  transfers between devices with their start and end apart: 53, of which 19 were waited for; matrix products, arithmetic and copies ran while one was open for 28% of the time, Pallas kernels for 11%

profile of v2, /device:TPU:0, one launch (start us, length us, event | category | flops | bytes accessed | tf_op | source)
XLA Modules:
  0.0 572.6 jit_solution(84014510791845189)
XLA Ops:
  7.3 5.1 collective-permute-start
  18.0 5.9 %collective-permute-done = bf16[256,1024]{1,0:T(8,128)(2,1)S(1)} collective-permute-done((bf16[256,1024]{1,0:T(8,128)(2,1)}, bf16[256,1024]{1,0:T(8,128)(2,1)S(1)}, u32[]{:S(2)}, u32[]{:S(2)}) %collective-permute-start) | collective-permute-done | bytes 524320 | tf_op jit(solution)/shard_map/ppermute | solution.py:560
  23.9 5.1 collective-permute-start.1
  32.8 6.4 %collective-permute-done.9 = bf16[1,128,1024]{2,1,0:T(8,128)(2,1)S(1)} collective-permute-done((bf16[1,128,1024]{2,1,0:T(8,128)(2,1)S(1)}, bf16[1,128,1024]{2,1,0:T(8,128)(2,1)S(1)}, u32[]{:S(2)}, u32[]{:S(2)}) %collective-permute-start.9) | collective-permute-done | bytes 262176 | tf_op jit(solution)/shard_map/ppermute | solution.py:549
  74.7 5.4 collective-permute-start.2
  89.8 9.0 %collective-permute-done.5 = bf16[256,1024]{1,0:T(8,128)(2,1)S(1)} collective-permute-done((bf16[256,1024]{1,0:T(8,128)(2,1)}, bf16[256,1024]{1,0:T(8,128)(2,1)S(1)}, u32[]{:S(2)}, u32[]{:S(2)}) %collective-permute-start.5) | collective-permute-done | bytes 524320 | tf_op jit(solution)/shard_map/ppermute | solution.py:561
  106.1 24.5 %collective-permute-done.19 = bf16[128,2304]{0,1:T(8,128)(2,1)} collective-permute-done((bf16[128,2304]{0,1:T(8,128)(2,1)}, bf16[128,2304]{0,1:T(8,128)(2,1)}, u32[]{:S(2)}, u32[]{:S(2)}) %collective-permute-start.19) | collective-permute-done | bytes 589856 | tf_op jit(solution)/shard_map/ppermute | solution.py:549
  133.1 4.0 collective-permute-start.12
  144.5 5.9 %fusion.3.raw_ref = f32[1024,1664]{1,0:T(8,128)} fusion(bf16[1024,1024]{1,0:T(8,128)(2,1)S(1)} %multiply_convert_fusion, bf16[1024,1920]{1,0:T(8,128)(2,1)S(1)} %copy-done.40), kind=kOutput, calls=%fused_computation.12 | convolution fusion | flops 3489660928 | bytes 12320768 | tf_op jit(solution)/shard_map/dot_general | solution.py:544
  150.4 29.4 %mixer_forward.1 = (bf16[1024,256]{1,0:T(8,128)(2,1)}, f32[1024,1280]{1,0:T(8,128)}, f32[1024,256]{1,0:T(8,128)S(1)}, f32[32,128,128]{2,1,0:T(8,128)S(1)}, f32[3...) custom-call(f32[1024,1664]{1,0:T(8,128)} %fusion.3.raw_ref, ...), custom_call_target="tpu_custom_call" | custom-call | tf_op jit(solution)/shard_map/mixer_forward/pallas_call | solution.py:425
  181.8 4.1 all-to-all-start
  197.3 36.5 %collective-permute-done.16 = bf16[1024,256]{1,0:T(8,128)(2,1)S(1)} collective-permute-done((bf16[1024,256]{1,0:T(8,128)(2,1)}, bf16[1024,256]{1,0:T(8,128)(2,1)S(1)}, u32[]{:S(2)}, u32[]{:S(2)}) %collective-permute-start.16) | collective-permute-done | bytes 524320 | tf_op jit(solution)/shard_map/ppermute | solution.py:577
  246.5 9.1 %collective-permute-done.18 = bf16[256,1024]{1,0:T(8,128)(2,1)} collective-permute-done((bf16[256,1024]{1,0:T(8,128)(2,1)S(1)}, bf16[256,1024]{1,0:T(8,128)(2,1)}, u32[]{:S(2)}, u32[]{:S(2)}) %collective-permute-start.18) | collective-permute-done | bytes 524320 | tf_op jit(solution)/shard_map/ppermute | solution.py:549
  255.6 5.6 fusion.11
  276.7 4.2 multiply_convert_fusion.4
  282.0 4.2 fusion.9
  286.3 4.3 fusion.15
  297.9 7.7 %collective-permute-done.22 = bf16[256,1024]{1,0:T(8,128)(2,1)S(1)} collective-permute-done((bf16[256,1024]{1,0:T(8,128)(2,1)S(1)}, bf16[256,1024]{1,0:T(8,128)(2,1)S(1)}, u32[]{:S(2)}, u32[]{:S(2)}) %collective-permute-start.22) | collective-permute-done | bytes 524320 | tf_op jit(solution)/shard_map/ppermute | solution.py:549
  306.1 7.9 %collective-permute-done.20 = bf16[256,1024]{1,0:T(8,128)(2,1)S(1)} collective-permute-done((bf16[256,1024]{1,0:T(8,128)(2,1)S(1)}, bf16[256,1024]{1,0:T(8,128)(2,1)S(1)}, u32[]{:S(2)}, u32[]{:S(2)}) %collective-permute-start.20) | collective-permute-done | bytes 524320 | tf_op jit(solution)/shard_map/ppermute | solution.py:549
  328.6 3.9 copy.119
  341.4 33.9 %mixer_backward.1 = (bf16[1024,1664]{1,0:T(8,128)(2,1)}, f32[4,1280]{1,0:T(4,128)S(1)}, f32[1,128]{1,0:T(1,128)S(1)}, f32[1,128]{1,0:T(1,128)S(1)}) custom-call(bf16[1024,256]{1,0:T(8,128)(2,1)S(1)} %bitcast.273, f32[1024,1664]{1,0:T(8,128)} %fusion.3.raw_ref, f32[1024,16]{1,0:T(8,128)S(1)} %copy.100.aux_ref, f32[16,1,128]{2,1,0:T(1,128)S(1)} %bitcast.275, ...), custom_call_target="tpu_custom_call" | custom-call | tf_op jit(solution)/shard_map/mixer_backward/pallas_call | solution.py:481
  375.6 7.7 %multiply_reduce_fusion = (f32[1024]{0:T(1024)S(1)}, bf16[1024,1024]{1,0:T(8,128)(2,1)S(1)}) fusion(bf16[4,256,1024]{2,1,0:T(8,128)(2,1)} %copy-done.7, f32[1024]{0:T(1024)S(1)} %bitcast.318, bf16[1024,1664]{1,0:T(8,128)(2,1)} %get-tuple-element.47, bf16[1024,1920]{1,0:T(8,128)(2,1)} %copy-done.39), kind=kOutput, calls=%fused_computation.3 | convolution fusion | flops 3494902784 | bytes 11018240 | tf_op jit(solution)/shard_map/dot_general | solution.py:544
  391.5 4.2 collective-permute-start.37
  402.6 6.6 %convolution_convert_fusion.2 = bf16[8,128,1664]{2,1,0:T(8,128)(2,1)S(1)} fusion(bf16[8,128,1024]{2,1,0:T(8,128)(2,1)} %bitcast.289, bf16[1024,1664]{1,0:T(8,128)(2,1)} %get-tuple-element.47), kind=kOutput, calls=%fused_computation.8 | convolution fusion | flops 3491364864 | bytes 8912896 | tf_op jit(solution)/shard_map/dot_general | solution.py:544
  418.4 12.4 %collective-permute-done.32 = f32[184,128]{1,0:T(8,128)S(1)} collective-permute-done((f32[184,128]{1,0:T(8,128)S(1)}, f32[184,128]{1,0:T(8,128)S(1)}, u32[]{:S(2)}, u32[]{:S(2)}) %collective-permute-start.32) | collective-permute-done | bytes 94240 | tf_op jit(solution)/shard_map/ppermute | solution.py:549
  447.0 7.7 %collective-permute-start.23 = (bf16[256,1024]{1,0:T(8,128)(2,1)}, bf16[256,1024]{1,0:T(8,128)(2,1)S(1)}, u32[]{:S(2)}, u32[]{:S(2)}) collective-permute-start(bf16[256,1024]{1,0:T(8,128)(2,1)} %get-tuple-element.122), channel_id=1, source_target_pairs={{0,8},{1,9},{2,10},{3,11},{4,12},{5,13},{6,14},{7,15}} | collective-permute-start | bytes 1572872 | tf_op jit(solution)/shard_map/ppermute | solution.py:596
  458.4 7.9 %collective-permute-done.23 = bf16[256,1024]{1,0:T(8,128)(2,1)S(1)} collective-permute-done((bf16[256,1024]{1,0:T(8,128)(2,1)}, bf16[256,1024]{1,0:T(8,128)(2,1)S(1)}, u32[]{:S(2)}, u32[]{:S(2)}) %collective-permute-start.23) | collective-permute-done | bytes 524320 | tf_op jit(solution)/shard_map/ppermute | solution.py:596
  467.3 5.1 collective-permute-start.24
  478.8 3.9 copy.105
  501.5 4.8 collective-permute-done.35
  514.4 14.2 %collective-permute-done.36 = bf16[128,896]{0,1:T(8,128)(2,1)S(1)} collective-permute-done((bf16[128,896]{0,1:T(8,128)(2,1)S(1)}, bf16[128,896]{0,1:T(8,128)(2,1)S(1)}, u32[]{:S(2)}, u32[]{:S(2)}) %collective-permute-start.36) | collective-permute-done | bytes 229408 | tf_op jit(solution)/shard_map/ppermute | solution.py:549
  544.9 17.0 %collective-permute-done.46 = bf16[128,2304]{1,0:T(8,128)(2,1)S(1)} collective-permute-done((bf16[128,2304]{1,0:T(8,128)(2,1)}, bf16[128,2304]{1,0:T(8,128)(2,1)S(1)}, u32[]{:S(2)}, u32[]{:S(2)}) %collective-permute-start.46) | collective-permute-done | bytes 589856 | tf_op jit(solution)/shard_map/ppermute | solution.py:549
  (391 shorter events, 212.4 us)
Async XLA Ops:
  7.3 248.4 %all-gather.3.cloned.1.call-start = ((), (), s32[]{:S(2)}) async-start(), calls=%async_computation.4 | async-start | bytes 5308416 | tf_op jit(solution)/shard_map/all_gather | solution.py:713
  12.4 61.0 %collective-permute-start.3 = (bf16[256,1024]{1,0:T(8,128)(2,1)}, bf16[256,1024]{1,0:T(8,128)(2,1)S(1)}, u32[]{:S(2)}, u32[]{:S(2)}) collective-permute-start(bf16[256,1024]{1,0:T(8,128)(2,1)} %param.35), channel_id=1, source_target_pairs={{8,0},{16,8},{24,16},{9,1},{17,9},{25,17},{10,2},{18,10},{26,18},{... | collective-permute-start | bytes 1572872 | tf_op jit(solution)/shard_map/ppermute | solution.py:561
  23.9 50.9 %collective-permute-start.1 = (bf16[256,1024]{1,0:T(8,128)(2,1)S(1)}, bf16[256,1024]{1,0:T(8,128)(2,1)}, u32[]{:S(2)}, u32[]{:S(2)}) collective-permute-start(bf16[256,1024]{1,0:T(8,128)(2,1)S(1)} %collective-permute-done), channel_id=1, source_target_pairs={{0,8},{8,16},{16,24},{1,9},{9,17},{17,25},{2,10},{10,18},{18,26},{... | collective-permute-start | bytes 1572872 | tf_op jit(solution)/shard_map/ppermute | solution.py:560
  32.3 49.6 %collective-permute-start.7 = (bf16[2,128,896]{2,1,0:T(8,128)(2,1)}, bf16[2,128,896]{2,1,0:T(8,128)(2,1)S(1)}, u32[]{:S(2)}, u32[]{:S(2)}) collective-permute-start(bf16[2,128,896]{2,1,0:T(8,128)(2,1)} %pad_maximum_fusion.16), channel_id=1, source_target_pairs={{0,2},{1,3},{2,0},{3,1},{4,6},{5,7},{6,4},{7,5},{8,10},{9,11},{10,... | collective-permute-start | bytes 1376264 | tf_op jit(solution)/shard_map/ppermute | solution.py:549
  40.0 42.1 %collective-permute-start.10 = (bf16[2,128,1024]{2,1,0:T(8,128)(2,1)}, bf16[2,128,1024]{2,1,0:T(8,128)(2,1)S(1)}, u32[]{:S(2)}, u32[]{:S(2)}) collective-permute-start(bf16[2,128,1024]{2,1,0:T(8,128)(2,1)} %pad_maximum_fusion.14), channel_id=1, source_target_pairs={{0,4},{1,5},{2,6},{3,7},{4,0},{5,1},{6,2},{7,3},{8,12},{9,13},{10,... | collective-permute-start | bytes 1572872 | tf_op jit(solution)/shard_map/ppermute | solution.py:549
  104.2 157.1 %all-gather.5.cloned.1.call-start = ((), (), s32[]{:S(2)}) async-start(), calls=%async_computation.5 | async-start | bytes 5308416 | tf_op jit(solution)/shard_map/all_gather | solution.py:713
  104.2 26.4 %collective-permute-start.19 = (bf16[128,2304]{0,1:T(8,128)(2,1)}, bf16[128,2304]{0,1:T(8,128)(2,1)}, u32[]{:S(2)}, u32[]{:S(2)}) collective-permute-start(bf16[128,2304]{0,1:T(8,128)(2,1)} %fusion.49), channel_id=1, source_target_pairs={{0,16},{8,24},{16,0},{24,8},{1,17},{9,25},{17,1},{25,9},{2,18},{10... | collective-permute-start | bytes 1769480 | tf_op jit(solution)/shard_map/ppermute | solution.py:549
  130.6 114.0 %collective-permute-start.21 = (bf16[256,1024]{1,0:T(8,128)(2,1)}, bf16[256,1024]{1,0:T(8,128)(2,1)}, u32[]{:S(2)}, u32[]{:S(2)}) collective-permute-start(bf16[256,1024]{1,0:T(8,128)(2,1)} %param.36), channel_id=1, source_target_pairs={{0,8},{8,0},{16,24},{24,16},{1,9},{9,1},{17,25},{25,17},{2,10},{10... | collective-permute-start | bytes 1572872 | tf_op jit(solution)/shard_map/ppermute | solution.py:549
  133.1 52.9 %collective-permute-start.12 = (bf16[1024,256]{1,0:T(8,128)(2,1)}, bf16[1024,256]{1,0:T(8,128)(2,1)}, u32[]{:S(2)}, u32[]{:S(2)}) collective-permute-start(bf16[1024,256]{1,0:T(8,128)(2,1)} %slice.267), channel_id=1, source_target_pairs={{0,24},{1,25},{2,26},{3,27},{4,28},{5,29},{6,30},{7,31}} | collective-permute-start | bytes 1572872 | tf_op jit(solution)/shard_map/ppermute | solution.py:577
  137.1 52.2 %collective-permute-start.13 = (bf16[1024,256]{1,0:T(8,128)(2,1)}, bf16[1024,256]{1,0:T(8,128)(2,1)}, u32[]{:S(2)}, u32[]{:S(2)}) collective-permute-start(bf16[1024,256]{1,0:T(8,128)(2,1)} %slice.267), channel_id=1, source_target_pairs={{0,16},{8,24},{1,17},{9,25},{2,18},{10,26},{3,19},{11,27},{4,20},{... | collective-permute-start | bytes 1572872 | tf_op jit(solution)/shard_map/ppermute | solution.py:577
  139.2 53.4 %collective-permute-start.14 = (bf16[1024,256]{1,0:T(8,128)(2,1)}, bf16[1024,256]{1,0:T(8,128)(2,1)}, u32[]{:S(2)}, u32[]{:S(2)}) collective-permute-start(bf16[1024,256]{1,0:T(8,128)(2,1)} %slice.267), channel_id=1, source_target_pairs={{0,8},{8,16},{16,24},{1,9},{9,17},{17,25},{2,10},{10,18},{18,26},{... | collective-permute-start | bytes 1572872 | tf_op jit(solution)/shard_map/ppermute | solution.py:577
  141.7 53.8 %collective-permute-start.15 = (bf16[1024,256]{1,0:T(8,128)(2,1)}, bf16[1024,256]{1,0:T(8,128)(2,1)}, u32[]{:S(2)}, u32[]{:S(2)}) collective-permute-start(bf16[1024,256]{1,0:T(8,128)(2,1)} %slice.267), channel_id=1, source_target_pairs={{8,0},{16,8},{24,16},{9,1},{17,9},{25,17},{10,2},{18,10},{26,18},{... | collective-permute-start | bytes 1572872 | tf_op jit(solution)/shard_map/ppermute | solution.py:577
  181.8 53.7 %all-to-all-start = ((bf16[4,256,256]{2,1,0:T(8,128)(2,1)}), bf16[4,256,256]{2,1,0:T(8,128)(2,1)}, u32[]{:S(2)}, u32[]{:S(2)}) async-start(bf16[4,256,256]{2,1,0:T(8,128)(2,1)} %bitcast.57), calls=%async_computation | async-start | bytes 1048576 | tf_op jit(solution)/shard_map/all_to_all | solution.py:742
  185.9 352.2 %reduce-scatter.5.cloned.1.call-start = ((), (), s32[]{:S(2)}) async-start(), calls=%async_computation.7 | async-start | bytes 5308416 | tf_op jit(solution)/shard_map/reduce_scatter | solution.py:783
  186.0 47.8 %collective-permute-start.16 = (bf16[1024,256]{1,0:T(8,128)(2,1)}, bf16[1024,256]{1,0:T(8,128)(2,1)S(1)}, u32[]{:S(2)}, u32[]{:S(2)}) collective-permute-start(bf16[1024,256]{1,0:T(8,128)(2,1)} %slice.267), channel_id=1, source_target_pairs={{16,0},{24,8},{17,1},{25,9},{18,2},{26,10},{19,3},{27,11},{20,4},{... | collective-permute-start | bytes 1572872 | tf_op jit(solution)/shard_map/ppermute | solution.py:577
  189.3 45.3 %collective-permute-start.17 = (bf16[1024,256]{1,0:T(8,128)(2,1)}, bf16[1024,256]{1,0:T(8,128)(2,1)S(1)}, u32[]{:S(2)}, u32[]{:S(2)}) collective-permute-start(bf16[1024,256]{1,0:T(8,128)(2,1)} %slice.267), channel_id=1, source_target_pairs={{24,0},{25,1},{26,2},{27,3},{28,4},{29,5},{30,6},{31,7}} | collective-permute-start | bytes 1572872 | tf_op jit(solution)/shard_map/ppermute | solution.py:577
  326.7 218.2 %reduce-scatter.3.cloned.1.call-start = ((), (), s32[]{:S(2)}) async-start(), calls=%async_computation.6 | async-start | bytes 5308416 | tf_op jit(solution)/shard_map/reduce_scatter | solution.py:783
  391.5 53.1 %collective-permute-start.37 = (bf16[256,1024]{1,0:T(8,128)(2,1)S(1)}, bf16[256,1024]{1,0:T(8,128)(2,1)}, u32[]{:S(2)}, u32[]{:S(2)}) collective-permute-start(bf16[256,1024]{1,0:T(8,128)(2,1)S(1)} %copy-done.9), channel_id=1, source_target_pairs={{0,24},{1,25},{2,26},{3,27},{4,28},{5,29},{6,30},{7,31}} | collective-permute-start | bytes 1572872 | tf_op jit(solution)/shard_map/ppermute | solution.py:577
  395.7 51.3 %collective-permute-start.38 = (bf16[256,1024]{1,0:T(8,128)(2,1)S(1)}, bf16[256,1024]{1,0:T(8,128)(2,1)}, u32[]{:S(2)}, u32[]{:S(2)}) collective-permute-start(bf16[256,1024]{1,0:T(8,128)(2,1)S(1)} %copy-done.9), channel_id=1, source_target_pairs={{0,16},{8,24},{1,17},{9,25},{2,18},{10,26},{3,19},{11,27},{4,20},{... | collective-permute-start | bytes 1572872 | tf_op jit(solution)/shard_map/ppermute | solution.py:577
  397.8 57.9 %collective-permute-start.39 = (bf16[256,1024]{1,0:T(8,128)(2,1)S(1)}, bf16[256,1024]{1,0:T(8,128)(2,1)}, u32[]{:S(2)}, u32[]{:S(2)}) collective-permute-start(bf16[256,1024]{1,0:T(8,128)(2,1)S(1)} %copy-done.9), channel_id=1, source_target_pairs={{0,8},{8,16},{16,24},{1,9},{9,17},{17,25},{2,10},{10,18},{18,26},{... | collective-permute-start | bytes 1572872 | tf_op jit(solution)/shard_map/ppermute | solution.py:577
  400.3 67.1 %collective-permute-start.40 = (bf16[256,1024]{1,0:T(8,128)(2,1)S(1)}, bf16[256,1024]{1,0:T(8,128)(2,1)}, u32[]{:S(2)}, u32[]{:S(2)}) collective-permute-start(bf16[256,1024]{1,0:T(8,128)(2,1)S(1)} %copy-done.9), channel_id=1, source_target_pairs={{8,0},{16,8},{24,16},{9,1},{17,9},{25,17},{10,2},{18,10},{26,18},{... | collective-permute-start | bytes 1572872 | tf_op jit(solution)/shard_map/ppermute | solution.py:577
  439.3 37.9 %collective-permute-start.41 = (bf16[256,1024]{1,0:T(8,128)(2,1)S(1)}, bf16[256,1024]{1,0:T(8,128)(2,1)S(1)}, u32[]{:S(2)}, u32[]{:S(2)}) collective-permute-start(bf16[256,1024]{1,0:T(8,128)(2,1)S(1)} %copy-done.9), channel_id=1, source_target_pairs={{16,0},{24,8},{17,1},{25,9},{18,2},{26,10},{19,3},{27,11},{20,4},{... | collective-permute-start | bytes 1572872 | tf_op jit(solution)/shard_map/ppermute | solution.py:577
  444.6 32.6 %collective-permute-start.42 = (bf16[256,1024]{1,0:T(8,128)(2,1)S(1)}, bf16[256,1024]{1,0:T(8,128)(2,1)S(1)}, u32[]{:S(2)}, u32[]{:S(2)}) collective-permute-start(bf16[256,1024]{1,0:T(8,128)(2,1)S(1)} %copy-done.9), channel_id=1, source_target_pairs={{24,0},{25,1},{26,2},{27,3},{28,4},{29,5},{30,6},{31,7}} | collective-permute-start | bytes 1572872 | tf_op jit(solution)/shard_map/ppermute | solution.py:577
  447.0 19.3 %collective-permute-start.23 = (bf16[256,1024]{1,0:T(8,128)(2,1)}, bf16[256,1024]{1,0:T(8,128)(2,1)S(1)}, u32[]{:S(2)}, u32[]{:S(2)}) collective-permute-start(bf16[256,1024]{1,0:T(8,128)(2,1)} %get-tuple-element.122), channel_id=1, source_target_pairs={{0,8},{1,9},{2,10},{3,11},{4,12},{5,13},{6,14},{7,15}} | collective-permute-start | bytes 1572872 | tf_op jit(solution)/shard_map/ppermute | solution.py:596
  455.8 40.4 %collective-permute-start.26 = (bf16[256,1024]{1,0:T(8,128)(2,1)}, bf16[256,1024]{1,0:T(8,128)(2,1)}, u32[]{:S(2)}, u32[]{:S(2)}) collective-permute-start(bf16[256,1024]{1,0:T(8,128)(2,1)} %get-tuple-element.123), channel_id=1, source_target_pairs={{24,16},{25,17},{26,18},{27,19},{28,20},{29,21},{30,22},{31,23}} | collective-permute-start | bytes 1572872 | tf_op jit(solution)/shard_map/ppermute | solution.py:597
  466.3 23.0 %collective-permute-start.34 = (bf16[2,2,128,896]{2,3,0,1:T(8,128)(2,1)}, bf16[2,2,128,896]{2,3,0,1:T(8,128)(2,1)}, u32[]{:S(2)}, u32[]{:S(2)}) collective-permute-start(bf16[2,2,128,896]{2,3,0,1:T(8,128)(2,1)} %bitcast.96), channel_id=1, source_target_pairs={{0,1},{1,0},{2,3},{3,2},{4,5},{5,4},{6,7},{7,6},{8,9},{9,8},{10,11... | collective-permute-start | bytes 2752520 | tf_op jit(solution)/shard_map/ppermute | solution.py:549
  467.3 28.9 %collective-permute-start.24 = (bf16[256,1024]{1,0:T(8,128)(2,1)}, bf16[256,1024]{1,0:T(8,128)(2,1)}, u32[]{:S(2)}, u32[]{:S(2)}) collective-permute-start(bf16[256,1024]{1,0:T(8,128)(2,1)} %fusion.44), channel_id=1, source_target_pairs={{0,8},{8,16},{1,9},{9,17},{2,10},{10,18},{3,11},{11,19},{4,12},{12... | collective-permute-start | bytes 1572872 | tf_op jit(solution)/shard_map/ppermute | solution.py:596
  489.3 18.1 %collective-permute-start.43 = (bf16[2,2,128,1024]{2,3,1,0:T(8,128)(2,1)}, bf16[2,2,128,1024]{2,3,1,0:T(8,128)(2,1)}, u32[]{:S(2)}, u32[]{:S(2)}) collective-permute-start(bf16[2,2,128,1024]{2,3,1,0:T(8,128)(2,1)} %bitcast.291), channel_id=1, source_target_pairs={{0,1},{1,0},{2,3},{3,2},{4,5},{5,4},{6,7},{7,6},{8,9},{9,8},{10,11... | collective-permute-start | bytes 3145736 | tf_op jit(solution)/shard_map/ppermute | solution.py:549
  499.4 34.4 %collective-permute-start.25 = (bf16[256,1024]{1,0:T(8,128)(2,1)}, bf16[256,1024]{1,0:T(8,128)(2,1)}, u32[]{:S(2)}, u32[]{:S(2)}) collective-permute-start(bf16[256,1024]{1,0:T(8,128)(2,1)} %get-tuple-element.120), channel_id=1, source_target_pairs={{0,8},{8,16},{16,24},{1,9},{9,17},{17,25},{2,10},{10,18},{18,26},{... | collective-permute-start | bytes 1572872 | tf_op jit(solution)/shard_map/ppermute | solution.py:596
  509.9 19.5 %collective-permute-start.44 = (bf16[2,128,1024]{1,2,0:T(8,128)(2,1)}, bf16[2,128,1024]{1,2,0:T(8,128)(2,1)}, u32[]{:S(2)}, u32[]{:S(2)}) collective-permute-start(bf16[2,128,1024]{1,2,0:T(8,128)(2,1)} %fusion.50), channel_id=1, source_target_pairs={{0,4},{1,5},{2,6},{3,7},{4,0},{5,1},{6,2},{7,3},{8,12},{9,13},{10,... | collective-permute-start | bytes 1572872 | tf_op jit(solution)/shard_map/ppermute | solution.py:549
  513.1 20.8 %collective-permute-start.28 = (bf16[256,1024]{1,0:T(8,128)(2,1)}, bf16[256,1024]{1,0:T(8,128)(2,1)}, u32[]{:S(2)}, u32[]{:S(2)}) collective-permute-start(bf16[256,1024]{1,0:T(8,128)(2,1)} %fusion.43), channel_id=1, source_target_pairs={{8,0},{16,8},{24,16},{9,1},{17,9},{25,17},{10,2},{18,10},{26,18},{... | collective-permute-start | bytes 1572872 | tf_op jit(solution)/shard_map/ppermute | solution.py:597
  538.2 23.7 %collective-permute-start.46 = (bf16[128,2304]{1,0:T(8,128)(2,1)}, bf16[128,2304]{1,0:T(8,128)(2,1)S(1)}, u32[]{:S(2)}, u32[]{:S(2)}) collective-permute-start(bf16[128,2304]{1,0:T(8,128)(2,1)} %reduce-scatter.5.cloned.1.call-done), channel_id=1, source_target_pairs={{0,16},{8,24},{16,0},{24,8},{1,17},{9,25},{17,1},{25,9},{2,18},{10... | collective-permute-start | bytes 1769480 | tf_op jit(solution)/shard_map/ppermute | solution.py:549
  (79 other events, 1193.3 us)
Sparse Core Ops, SparseCore 0:
  104.3 38.2 all-gather.2
  144.4 39.7 all-gather.4
  276.8 51.1 reduce-scatter.4
  390.6 51.6 reduce-scatter.2
